TPU v7x, 512 devices: a whole 4x8x8 slice. The times are simulated.
512 devices in a mesh: rep: 64 (over z, y), ch: 8 (over x, core).
Axes of the slice: x: 4, y: 8, z: 8, core: 2. Of those that a mesh axis runs over, the one named last changes fastest.
Arguments:
- inner_input: bfloat16 [384, 10, 8192], P('rep', None, 'ch'), may hold values from -6 to 6
- group_input: bfloat16 [384, 10, 8, 256], P('rep', None, 'ch'), may hold values from -6 to 6
- gate_input: bfloat16 [384, 10, 8192], P('rep', None, 'ch'), may hold values from -6 to 6
- step_size: float32 [384, 10, 128], P('rep', None, 'ch'), may hold values from -6 to 6
- scan_state: bfloat16 [384, 128, 64, 128], P('rep', 'ch'), may hold values from -6 to 6
- conv_inner: bfloat16 [384, 3, 8192], P('rep', None, 'ch'), may hold values from -6 to 6
- conv_group: bfloat16 [384, 3, 8, 256], P('rep', None, 'ch'), may hold values from -6 to 6
- prefix_scan: bfloat16 [128, 128, 64, 128], P('rep', 'ch'), may hold values from -6 to 6
- prefix_inner: bfloat16 [128, 3, 8192], P('rep', None, 'ch'), may hold values from -6 to 6
- prefix_group: bfloat16 [128, 3, 8, 256], P('rep', None, 'ch'), may hold values from -6 to 6
- inner_kernel: bfloat16 [4, 8192], P(None, 'ch'), may hold values from -3 to 3
- inner_bias: bfloat16 [8192], P('ch'), may hold values from -3 to 3
- group_kernel: bfloat16 [4, 8, 256], P(None, 'ch'), may hold values from -3 to 3
- group_bias: bfloat16 [8, 256], P('ch'), may hold values from -3 to 3
- decay_rate: float32 [128], P('ch'), may hold values from 0.02 to 2
- step_bias: float32 [128], P('ch'), may hold values from -3 to 0
- skip_gain: float32 [128], P('ch'), may hold values from 0.5 to 1.5
- norm_gain: float32 [8192], P('ch'), may hold values from 0.5 to 1.5
- event_prefix: int32 [4], replicated, may hold values from 0 to 127, as said below
- slot_event: int32 [384], P('rep'), may hold values from -1 to 3, as said below
- moved_slot: int32 [64], P('rep'), may hold values from 0 to 5
Outputs:
- layer_output: bfloat16 [384, 10, 8192], P('rep', None, 'ch')
- final_scan: bfloat16 [384, 128, 64, 128], P('rep', 'ch')
- final_inner: bfloat16 [384, 3, 8192], P('rep', None, 'ch')
- final_group: bfloat16 [384, 3, 8, 256], P('rep', None, 'ch')
Inputs may be any that keep to these rules, and one draw needn't show every extreme that they name: `event_prefix`: distinct rows of the cached prefixes. `slot_event`: every value from -1 to 3 occurs.
All inputs are finite; a program needn't handle non-finite values.
Results may differ from a plain program's by a relative error of at most 0.0015.
Values may be sent and summed in bfloat16 or wider, within the bound.
A program may use at most 64 MiB of HBM per device.

v0:
```python
import jax
import jax.numpy as jnp
from jax import lax
from jax.sharding import PartitionSpec as P

N = 128


epsilon = 1e-05


def from_root(value, axis, source):
    kept = jnp.where(lax.axis_index(axis) == source, value, 0).astype(value.dtype)
    return lax.psum(kept, axis)


def shifted(x, axis, by):
    count = lax.axis_size(axis)
    return lax.ppermute(x, axis, [(i, (i + by) % count) for i in range(count)])


def conv_apply(tail_cache, inputs, kernel, offset):
    step_count = inputs.shape[1]
    joined = jnp.concatenate([tail_cache.astype(jnp.float32), inputs.astype(jnp.float32)], axis=1)
    summed = offset.astype(jnp.float32)
    for tap_index in range(kernel.shape[0]):
        summed = (
            summed
            + kernel[tap_index].astype(jnp.float32) * joined[:, tap_index : tap_index + step_count]
        )
    return (jax.nn.silu(summed), joined[:, step_count:])


def run_scan(start, inner_act, group_act, step_size, decay_rate, step_bias, skip_gain, state_width):
    slot_count, step_count, row_width = inner_act.shape
    head_count = step_size.shape[2]
    group_count = group_act.shape[2]
    head_size = row_width // head_count
    carried = start
    outputs = []
    for moment in range(step_count):
        step_value = jax.nn.softplus(step_size[:, moment] + step_bias)
        retain = jnp.exp(-step_value * decay_rate)
        values = inner_act[:, moment].reshape(slot_count, head_count, head_size)
        keys_in = jnp.repeat(
            group_act[:, moment, :, :state_width], head_count // group_count, axis=1
        )
        readout = jnp.repeat(
            group_act[:, moment, :, state_width:], head_count // group_count, axis=1
        )
        carried = (
            retain[:, :, None, None] * carried
            + (step_value[:, :, None] * values)[:, :, :, None] * keys_in[:, :, None, :]
        )
        result = (
            jnp.einsum("shpn,shn->shp", carried, readout, precision=lax.Precision.HIGHEST)
            + skip_gain[:, None] * values
        )
        outputs.append(result.reshape(slot_count, row_width))
    return (jnp.stack(outputs, axis=1), carried)


def on_device(
    inner_input,
    group_input,
    gate_input,
    step_size,
    scan_state,
    conv_inner,
    conv_group,
    prefix_scan,
    prefix_inner,
    prefix_group,
    inner_kernel,
    inner_bias,
    group_kernel,
    group_bias,
    decay_rate,
    step_bias,
    skip_gain,
    norm_gain,
    event_prefix,
    slot_event,
    moved_slot,
):
    slot_count = inner_input.shape[0]
    prefix_count = prefix_scan.shape[0]
    event_count = event_prefix.shape[0]
    local_rows = event_prefix % prefix_count
    owners = event_prefix // prefix_count
    list_scan = []
    list_inner = []
    list_group = []
    for position in range(event_count):
        local_row = local_rows[position]
        own_scan = lax.dynamic_index_in_dim(prefix_scan, local_row, 0, False)
        own_inner = lax.dynamic_index_in_dim(prefix_inner, local_row, 0, False)
        own_group = lax.dynamic_index_in_dim(prefix_group, local_row, 0, False)
        got_scan, got_inner, got_group = (
            from_root(own_scan, "rep", owners[position]),
            from_root(own_inner, "rep", owners[position]),
            from_root(own_group, "rep", owners[position]),
        )
        list_scan.append(got_scan)
        list_inner.append(got_inner)
        list_group.append(got_group)
    shared_scan = jnp.stack(list_scan)
    shared_inner = jnp.stack(list_inner)
    shared_group = jnp.stack(list_group)
    leaving = moved_slot[0]
    out_scan = lax.dynamic_index_in_dim(scan_state, leaving, 0, False)
    out_inner = lax.dynamic_index_in_dim(conv_inner, leaving, 0, False)
    out_group = lax.dynamic_index_in_dim(conv_group, leaving, 0, False)
    came_scan, came_inner, came_group = shifted((out_scan, out_inner, out_group), "rep", 1)
    prefix_hit = slot_event >= 0
    which_event = jnp.maximum(slot_event, 0)
    moved_here = jnp.arange(slot_count, dtype=jnp.int32) == leaving

    def select_start(own_part, came_part, shared_part):
        shape_tail = (slot_count,) + (1,) * (own_part.ndim - 1)
        chosen = jnp.where(moved_here.reshape(shape_tail), came_part[None], own_part)
        return jnp.where(prefix_hit.reshape(shape_tail), shared_part[which_event], chosen)

    start_scan = select_start(scan_state, came_scan, shared_scan).astype(jnp.float32)
    start_inner = select_start(conv_inner, came_inner, shared_inner)
    start_group = select_start(conv_group, came_group, shared_group)
    inner_act, tail_inner = conv_apply(start_inner, inner_input, inner_kernel, inner_bias)
    group_act, tail_group = conv_apply(start_group, group_input, group_kernel, group_bias)
    outputs, carried = run_scan(
        start_scan, inner_act, group_act, step_size, decay_rate, step_bias, skip_gain, N
    )
    gated = outputs * jax.nn.silu(gate_input.astype(jnp.float32))
    local_groups = group_input.shape[2]
    grouped = gated.reshape(
        gated.shape[0], gated.shape[1], local_groups, gated.shape[2] // local_groups
    )
    norm_scale = lax.rsqrt(jnp.mean(grouped * grouped, axis=-1, keepdims=True) + epsilon)
    normed = (grouped * norm_scale).reshape(gated.shape) * norm_gain
    return (
        normed.astype(jnp.bfloat16),
        carried.astype(jnp.bfloat16),
        tail_inner.astype(jnp.bfloat16),
        tail_group.astype(jnp.bfloat16),
    )


def solution(mesh):
    placed = (
        P("rep", None, "ch"),
        P("rep", None, "ch", None),
        P("rep", None, "ch"),
        P("rep", None, "ch"),
        P("rep", "ch", None, None),
        P("rep", None, "ch"),
        P("rep", None, "ch", None),
        P("rep", "ch", None, None),
        P("rep", None, "ch"),
        P("rep", None, "ch", None),
        P(None, "ch"),
        P("ch"),
        P(None, "ch", None),
        P("ch", None),
        P("ch"),
        P("ch"),
        P("ch"),
        P("ch"),
        P(),
        P("rep"),
        P("rep"),
    )
    return jax.shard_map(
        on_device,
        mesh=mesh,
        in_specs=placed,
        out_specs=(
            P("rep", None, "ch"),
            P("rep", "ch", None, None),
            P("rep", None, "ch"),
            P("rep", None, "ch", None),
        ),
        check_vma=False,
    )
```

profile of v0, /device:TPU:6, one launch (start us, length us, event | category | flops | bytes accessed | tf_op | source)
XLA Modules:
  0.0 429.2 jit_solution(5048661160661196294)
XLA Ops:
  8.2 0.7 dynamic-slice_bitcast_fusion.1
  8.9 3.5 collective-permute-start.1
  13.0 3.5 collective-permute-start.2
  16.5 1.0 dynamic-slice_bitcast_fusion
  17.5 3.5 collective-permute-start
  32.7 2.3 dynamic-slice_select_fusion.3
  36.0 281.4 %all-reduce = (bf16[1,3,1,256]{3,1,0,2:T(4,128)(2,1)S(1)}, bf16[1,3,1,256]{3,1,0,2:T(4,128)(2,1)S(1)}, bf16[1,3,1,256]{3,1,0,2:T(4,128)(2,1)S(1)}, bf16[1,3,1,25...) all-reduce(bf16[1,3,1,256]{3,1,0,2:T(4,128)(2,1)S(1)} %copy_select_, ...), channel_id=1, replica_groups=mesh['rep'=64,'ch'=8] {'rep'}, use_global_device_ids=true, to_apply=%region_11.12 | all-reduce | flops 15360 | bytes 61440 | tf_op jit(solution)/shard_map/psum | solution.py:14
  322.6 0.7 broadcast_multiply_fusion
  323.3 0.7 broadcast_multiply_fusion.1
  328.9 1.3 pad_maximum_fusion
  330.2 1.0 gather_fusion
  331.2 0.7 copy-done.8
  332.0 14.0 %fusion.5 = (bf16[6,16,64,128]{3,2,1,0:T(8,128)(2,1)}, f32[6,16,64,128]{3,2,1,0:T(8,128)S(1)}, bf16[6,16,64,128]{3,2,1,0:T(8,128)(2,1)S(1)}) fusion(f32[6,128]{1,0:T(8,128)} %get-tuple-element.54, f32[6,16,64]{2,1,0:T(8,128)} %broadcast_multiply_fusion, f32[6,16]{1,0:T(8,128)} %get-tuple-element.88, f32[6,128]{1,0:T(8,128)} %get-tuple-element.56, ...), kind=kLoop, calls=%fused_computation.18 | loop fusion | flops 26738688 | bytes 9979660 | tf_op jit(solution)/shard_map/convert_element_type | solution.py:141
  346.1 8.9 %fusion.56 = f32[6,16,1,64]{3,2,1,0:T(1,128)S(1)} fusion(f32[6,16,128,1]{2,3,1,0:T(1,128)S(1)} %bitcast.206, f32[6,128]{1,0:T(8,128)S(1)} %copy-done.31, f32[6,16,64]{2,1,0:T(8,128)S(1)} %copy-done.11, f32[6,16]{1,0:T(8,128)S(1)} %copy-done.25, f32[6,128]{1,0:T(8,128)S(1)} %copy-done.32, f32[6,16,64]{2,1,0:T(8,128)S(1)} %copy-done.12, ...), kind=kOutput, calls=%fused_computation.213 | convolution fusion | flops 18874368 | bytes 3331584 | tf_op jit(solution)/shard_map/shpn,shn->shp/dot_general | solution.py:56
  355.0 8.0 %fusion.4 = f32[6,16,1,64]{3,2,1,0:T(1,128)S(1)} fusion(f32[6,16,128,1]{2,3,1,0:T(1,128)S(1)} %bitcast.207, f32[6,128]{1,0:T(8,128)S(1)} %copy-done.32, f32[6,16,64]{2,1,0:T(8,128)S(1)} %copy-done.12, f32[6,16]{1,0:T(8,128)S(1)} %copy-done.24, f32[6,16,64,128]{3,2,1,0:T(8,128)S(1)} %get-tuple-element.17, f32[6,128]{1,0:T(8,128)S(1)} %copy-done.33, ...), kind=kOutput, calls=%fused_computation.17 | convolution fusion | flops 16515072 | bytes 3303552 | tf_op jit(solution)/shard_map/shpn,shn->shp/dot_general | solution.py:56
  363.0 7.1 %fusion.29 = f32[6,16,1,64]{3,2,1,0:T(1,128)S(1)} fusion(f32[6,16,128,1]{2,3,1,0:T(1,128)S(1)} %bitcast.208, f32[6,16,64,128]{3,2,1,0:T(8,128)S(1)} %get-tuple-element.17, f32[6,128]{1,0:T(8,128)S(1)} %copy-done.33, f32[6,16,64]{2,1,0:T(8,128)S(1)} %copy-done.13, f32[6,16]{1,0:T(8,128)S(1)} %get-tuple-element.82, f32[6,128]{1,0:T(8,128)S(1)} %get-tuple-element.62, ...), kind=kOutput, calls=%fused_computation.44 | convolution fusion | flops 14155776 | bytes 3275520 | tf_op jit(solution)/shard_map/shpn,shn->shp/dot_general | solution.py:56
  370.2 5.2 %fusion.3 = f32[6,16,1,64]{3,2,1,0:T(1,128)S(1)} fusion(f32[6,16,128,1]{2,3,1,0:T(1,128)S(1)} %bitcast.192, f32[6,16,64,128]{3,2,1,0:T(8,128)S(1)} %get-tuple-element.17, f32[6,128]{1,0:T(8,128)S(1)} %get-tuple-element.62, f32[6,16,64]{2,1,0:T(8,128)S(1)} %broadcast_multiply_fusion.4, f32[6,16]{1,0:T(8,128)S(1)} %get-tuple-element.80), kind=kOutput, calls=%fused_computation.16 | convolution fusion | flops 11796480 | bytes 3247488 | tf_op jit(solution)/shard_map/shpn,shn->shp/dot_general | solution.py:56
  375.6 9.1 %fusion.2 = f32[6,16,1,64]{3,2,1,0:T(1,128)S(1)} fusion(f32[6,16,128,1]{2,3,1,0:T(1,128)S(1)} %bitcast.203, f32[6,128]{1,0:T(8,128)S(1)} %copy-done.36, f32[6,16,64]{2,1,0:T(8,128)S(1)} %copy-done.16, f32[6,16]{1,0:T(8,128)S(1)} %copy-done.29, bf16[6,16,64,128]{3,2,1,0:T(8,128)(2,1)S(1)} %get-tuple-element.18, f32[6,128]{1,0:T(8,128)S(1)} %copy-done.35, ...), kind=kOutput, calls=%fused_computation.15 | convolution fusion | flops 19660800 | bytes 1758720 | tf_op jit(solution)/shard_map/shpn,shn->shp/dot_general | solution.py:56
  384.7 8.0 %fusion.28 = f32[6,16,1,64]{3,2,1,0:T(1,128)S(1)} fusion(f32[6,16,128,1]{2,3,1,0:T(1,128)S(1)} %bitcast.204, bf16[6,16,64,128]{3,2,1,0:T(8,128)(2,1)S(1)} %get-tuple-element.18, f32[6,128]{1,0:T(8,128)S(1)} %copy-done.35, f32[6,16,64]{2,1,0:T(8,128)S(1)} %copy-done.15, f32[6,16]{1,0:T(8,128)S(1)} %copy-done.28, f32[6,128]{1,0:T(8,128)S(1)} %copy-done.34, ...), kind=kOutput, calls=%fused_computation.42 | convolution fusion | flops 17301504 | bytes 1730688 | tf_op jit(solution)/shard_map/shpn,shn->shp/dot_general | solution.py:56
  392.7 7.0 %fusion.1 = f32[6,16,1,64]{3,2,1,0:T(1,128)S(1)} fusion(f32[6,16,128,1]{2,3,1,0:T(1,128)S(1)} %bitcast.205, bf16[6,16,64,128]{3,2,1,0:T(8,128)(2,1)S(1)} %get-tuple-element.18, f32[6,128]{1,0:T(8,128)S(1)} %copy-done.34, f32[6,16,64]{2,1,0:T(8,128)S(1)} %copy-done.14, f32[6,16]{1,0:T(8,128)S(1)} %copy-done.27, f32[6,128]{1,0:T(8,128)S(1)} %copy-done.37, ...), kind=kOutput, calls=%fused_computation.14 | convolution fusion | flops 14942208 | bytes 1702656 | tf_op jit(solution)/shard_map/shpn,shn->shp/dot_general | solution.py:56
  399.8 5.0 %fusion.60 = f32[6,16,1,64]{3,2,1,0:T(1,128)S(1)} fusion(f32[6,16,64,128]{3,2,1,0:T(8,128)S(1)} %get-tuple-element.17, f32[6,16,128,1]{2,3,1,0:T(1,128)S(1)} %bitcast.193), kind=kOutput, calls=%fused_computation.217 | convolution fusion | flops 9437184 | bytes 3219456 | tf_op jit(solution)/shard_map/shpn,shn->shp/dot_general | solution.py:56
  404.8 10.0 %fusion.6 = f32[6,16,1,64]{3,2,1,0:T(1,128)S(1)} fusion(f32[6,16,128,1]{2,3,1,0:T(1,128)S(1)} %bitcast.201, f32[6,128]{1,0:T(8,128)S(1)} %copy-done.30, f32[6,16,64]{2,1,0:T(8,128)S(1)} %copy-done.10, f32[6,16]{1,0:T(8,128)S(1)} %copy-done.26, f32[6,128]{1,0:T(8,128)S(1)} %copy-done.31, f32[6,16,64]{2,1,0:T(8,128)S(1)} %copy-done.11, ...), kind=kOutput, calls=%fused_computation.19 | convolution fusion | flops 21233664 | bytes 3359616 | tf_op jit(solution)/shard_map/shpn,shn->shp/dot_general | solution.py:56
  415.1 5.2 %fusion = f32[6,16,1,64]{3,2,1,0:T(1,128)S(1)} fusion(f32[6,16,128,1]{2,3,1,0:T(1,128)S(1)} %bitcast.202, bf16[6,16,64,128]{3,2,1,0:T(8,128)(2,1)S(1)} %get-tuple-element.18, f32[6,128]{1,0:T(8,128)S(1)} %copy-done.37, f32[6,16,64]{2,1,0:T(8,128)S(1)} %copy-done.9, f32[6,16]{1,0:T(8,128)S(1)} %get-tuple-element.37), kind=kOutput, calls=%fused_computation.13 | convolution fusion | flops 12582912 | bytes 1674624 | tf_op jit(solution)/shard_map/shpn,shn->shp/dot_general | solution.py:56
  421.5 0.8 multiply_convert_fusion
  (216 shorter events, 14.4 us)
Async XLA Ops:
  7.2 314.3 %copy-start.19 = (bf16[6,3,1024]{2,1,0:T(4,128)(2,1)S(1)}, bf16[6,3,1024]{2,1,0:T(4,128)(2,1)}, u32[]{:S(2)}) copy-start(bf16[6,3,1024]{2,1,0:T(4,128)(2,1)} %param.26) | copy-start | bytes 110596
  7.2 312.9 %copy-start.23 = (bf16[6,3,1,256]{3,1,2,0:T(4,128)(2,1)S(1)}, bf16[6,3,1,256]{3,1,2,0:T(4,128)(2,1)}, u32[]{:S(2)}) copy-start(bf16[6,3,1,256]{3,1,2,0:T(4,128)(2,1)} %param.27) | copy-start | bytes 27652
  7.2 27.8 %copy-start.58 = (s32[6]{0:T(128)S(1)}, s32[6]{0:T(128)}, u32[]{:S(2)}) copy-start(s32[6]{0:T(128)} %param.40) | copy-start | bytes 76
  7.2 27.8 %copy-start.17 = (bf16[2,3,1024]{2,0,1:T(2,128)(2,1)S(1)}, bf16[2,3,1024]{2,0,1:T(2,128)(2,1)}, u32[]{:S(2)}) copy-start(bf16[2,3,1024]{2,0,1:T(2,128)(2,1)} %param.29) | copy-start | bytes 36868
  7.2 27.9 %copy-start.20 = (bf16[2,3,1,256]{3,0,2,1:T(2,128)(2,1)S(1)}, bf16[2,3,1,256]{3,0,2,1:T(2,128)(2,1)}, u32[]{:S(2)}) copy-start(bf16[2,3,1,256]{3,0,2,1:T(2,128)(2,1)} %param.30) | copy-start | bytes 9220
  7.2 28.0 %copy-start.22 = (bf16[4,1024]{1,0:T(4,128)(2,1)S(1)}, bf16[4,1024]{1,0:T(4,128)(2,1)}, u32[]{:S(2)}) copy-start(bf16[4,1024]{1,0:T(4,128)(2,1)} %param.31) | copy-start | bytes 24580
  7.2 28.1 %copy-start.48 = (bf16[4,1,256]{2,0,1:T(4,128)(2,1)S(1)}, bf16[4,1,256]{2,0,1:T(4,128)(2,1)}, u32[]{:S(2)}) copy-start(bf16[4,1,256]{2,0,1:T(4,128)(2,1)} %param.33) | copy-start | bytes 6148
  7.2 28.1 %copy-start.21 = (f32[6,10,16]{2,0,1:T(8,128)S(1)}, f32[6,10,16]{2,0,1:T(8,128)}, u32[]{:S(2)}) copy-start(f32[6,10,16]{2,0,1:T(8,128)} %param.24) | copy-start | bytes 11524
  7.3 28.1 %copy-start.56 = (f32[16]{0:T(128)S(1)}, f32[16]{0:T(128)}, u32[]{:S(2)}) copy-start(f32[16]{0:T(128)} %param.35) | copy-start | bytes 196
  7.3 28.1 %copy-start.57 = (f32[16]{0:T(128)S(1)}, f32[16]{0:T(128)}, u32[]{:S(2)}) copy-start(f32[16]{0:T(128)} %param.36) | copy-start | bytes 196
  7.3 310.2 %copy-start.7 = (bf16[6,10,1024]{2,0,1:T(8,128)(2,1)S(1)}, bf16[6,10,1024]{2,0,1:T(8,128)(2,1)}, u32[]{:S(2)}) copy-start(bf16[6,10,1024]{2,0,1:T(8,128)(2,1)} %param.21) | copy-start | bytes 368644
  7.3 311.5 %slice-start = ((bf16[6,10,1024]{2,0,1:T(8,128)(2,1)}), bf16[6,3,1024]{2,0,1:T(8,128)(2,1)S(1)}, s32[]{:S(2)}) async-start(bf16[6,10,1024]{2,0,1:T(8,128)(2,1)} %param.21), calls=%async_computation.1 | async-start | bytes 98304 | tf_op jit(solution)/shard_map/slice | solution.py:31
  7.3 310.2 %copy-start.18 = (bf16[6,10,1,256]{3,0,2,1:T(8,128)(2,1)S(1)}, bf16[6,10,1,256]{3,0,2,1:T(8,128)(2,1)}, u32[]{:S(2)}) copy-start(bf16[6,10,1,256]{3,0,2,1:T(8,128)(2,1)} %param.22) | copy-start | bytes 92164
  7.3 312.1 %slice-start.1 = ((bf16[6,10,1,256]{3,0,2,1:T(8,128)(2,1)}), bf16[6,3,1,256]{3,0,2,1:T(8,128)(2,1)S(1)}, s32[]{:S(2)}) async-start(bf16[6,10,1,256]{3,0,2,1:T(8,128)(2,1)} %param.22), calls=%async_computation.2 | async-start | bytes 24576 | tf_op jit(solution)/shard_map/slice | solution.py:31
  7.3 310.2 %copy-start.54 = (bf16[1024]{0:T(1024)(128)(2,1)S(1)}, bf16[1024]{0:T(1024)(128)(2,1)}, u32[]{:S(2)}) copy-start(bf16[1024]{0:T(1024)(128)(2,1)} %param.32) | copy-start | bytes 6148
  7.3 311.4 %copy-start.55 = (bf16[1,256]{1,0:T(2,128)(2,1)S(1)}, bf16[1,256]{1,0:T(2,128)(2,1)}, u32[]{:S(2)}) copy-start(bf16[1,256]{1,0:T(2,128)(2,1)} %param.34) | copy-start | bytes 1540
  7.3 321.6 %all-reduce.4.cloned.1.call-start = ((), (), s32[]{:S(2)}) async-start(), calls=%async_computation | async-start | bytes 2097152 | tf_op jit(solution)/shard_map/psum | solution.py:14
  8.9 312.6 %collective-permute-start.1 = (bf16[3,1024]{1,0:T(4,128)(2,1)S(1)}, bf16[3,1024]{1,0:T(4,128)(2,1)S(1)}, u32[]{:S(2)}, u32[]{:S(2)}) collective-permute-start(bf16[3,1024]{1,0:T(4,128)(2,1)S(1)} %dynamic-slice_bitcast_fusion.1), channel_id=1, source_target_pairs={{0,8},{8,16},{16,24},{24,32},{32,40},{40,48},{48,56},{56,64},{64,7... | collective-permute-start | bytes 18440 | tf_op jit(solution)/shard_map/ppermute | solution.py:19
  13.0 307.0 %collective-permute-start.2 = (bf16[3,1,256]{2,0,1:T(4,128)(2,1)S(1)}, bf16[3,1,256]{2,0,1:T(4,128)(2,1)S(1)}, u32[]{:S(2)}, u32[]{:S(2)}) collective-permute-start(bf16[3,1,256]{2,0,1:T(4,128)(2,1)S(1)} %fusion.55), channel_id=1, source_target_pairs={{0,8},{8,16},{16,24},{24,32},{32,40},{40,48},{48,56},{56,64},{64,7... | collective-permute-start | bytes 4616 | tf_op jit(solution)/shard_map/ppermute | solution.py:19
  17.5 313.7 %collective-permute-start = (bf16[16,64,128]{2,1,0:T(8,128)(2,1)S(1)}, bf16[16,64,128]{2,1,0:T(8,128)(2,1)S(1)}, u32[]{:S(2)}, u32[]{:S(2)}) collective-permute-start(bf16[16,64,128]{2,1,0:T(8,128)(2,1)S(1)} %dynamic-slice_bitcast_fusion), channel_id=1, source_target_pairs={{0,8},{8,16},{16,24},{24,32},{32,40},{40,48},{48,56},{56,64},{64,7... | collective-permute-start | bytes 786440 | tf_op jit(solution)/shard_map/ppermute | solution.py:19
  35.2 286.6 %copy-start.49 = (pred[6]{0:T(512)(128)(4,1)}, pred[6]{0:T(512)(128)(4,1)S(1)}, u32[]{:S(2)}) copy-start(pred[6]{0:T(512)(128)(4,1)S(1)} %get-tuple-element.129) | copy-start | bytes 22
  35.3 286.6 %copy-start.50 = (pred[6]{0:T(512)(128)(4,1)}, pred[6]{0:T(512)(128)(4,1)S(1)}, u32[]{:S(2)}) copy-start(pred[6]{0:T(512)(128)(4,1)S(1)} %get-tuple-element.130) | copy-start | bytes 22
  331.9 14.1 %copy-start.24 = (f32[6,16]{1,0:T(8,128)S(1)}, f32[6,16]{1,0:T(8,128)}, u32[]{:S(2)}) copy-start(f32[6,16]{1,0:T(8,128)} %get-tuple-element.84) | copy-start | bytes 1156
  332.0 14.1 %copy-start.25 = (f32[6,16]{1,0:T(8,128)S(1)}, f32[6,16]{1,0:T(8,128)}, u32[]{:S(2)}) copy-start(f32[6,16]{1,0:T(8,128)} %get-tuple-element.86) | copy-start | bytes 1156
  (41 other events, 314.2 us)
Sparse Core Ops, SparseCore 0:
  35.1 162.2 all-reduce.3
where the time goes:
time: 430 us; the launch traced here: 429 us
  blocking collectives  281 us (65%)
  matrix products  73.4 us (17%)
  other arithmetic  27 us (6%)
  between operations  26.3 us (6%)
  local copies, waits for them, and re-layouts  10.5 us (2%)
  starting transfers between devices  10.5 us (2%)
    psum x1, blocking collectives, from_root(): return lax.psum(kept, axis)  281 us
    dot_general x10, matrix products, run_scan(): jnp.einsum('shpn,shn->shp', carried, readout, precision=lax.Precision.HIG...  73.4 us
    convert_element_type x1, other arithmetic, on_device(): carried.astype(jnp.bfloat16)  14 us
    ppermute x3, starting transfers between devices, shifted(): return lax.ppermute(x, axis, [(i, (i + by) % count) for i in range(count)])  10.4 us
  transfers between devices with their start and end apart: 4, of which 0 were waited for; matrix products, arithmetic and copies ran while one was open for 5% of the time, Pallas kernels for 0%

commit v1 on v0

v1 whole, which is shorter than its diff:
```python
import functools

import jax
import jax.numpy as jnp
from jax import lax
from jax.experimental import pallas as pl
from jax.experimental.pallas import tpu as pltpu
from jax.sharding import PartitionSpec as P

MESH = pl.DeviceIdType.MESH
BF16 = jnp.bfloat16
F32 = jnp.float32
EPSILON = 1e-05


def silu(v):
    return v / (1.0 + jnp.exp(-v))


def split2(v):
    high = v.astype(BF16)
    low = (v - high.astype(F32)).astype(BF16)
    return high, low


class Stream:
    def __init__(self, index, n, pos1, pos2, peer1, peer2, cand, red, cand2, candc, redc, candc2, conv, sems):
        self.index, self.n = index, n
        self.pos1, self.pos2 = pos1, pos2
        self.peer1, self.peer2 = peer1, peer2
        self.cand, self.red, self.cand2 = cand, red, cand2
        self.candc, self.redc, self.candc2 = candc, redc, candc2
        self.conv = conv
        self.sems = sems


def kernel(
    n, slots, pref, events, steps, heads, hsize, state,
    inner_ref, group_ref, gate_ref, dt_ref, scan_hbm, cinner_ref, cgroup_ref, pscan_hbm, pinner_ref, pgroup_ref,
    ikern_ref, ibias_ref, gkern_ref, gbias_ref, decay_ref, dbias_ref, skip_ref, gain_ref, ep_ref, se_ref, mv_ref,
    out_ref, fin_ref,
    pool, stage, cand_a, cand_b, red_a, red_b, cand2_a, cand2_b,
    pkf, pkb, candc_a, candc_b, redc_a, redc_b, candc2_a, candc2_b, conv_a, conv_b, camec, ucf,
    join, joing, xs, gs, dts, ms, us, ys, es,
    load_sem, s1, r1, s2, r2, s3, r3, s4, r4, sc1, rc1, sc2, rc2, sc3, rc3, sc4, rc4, sm, rm,
):
    rep = lax.axis_index("rep")
    total = n * n
    py = lax.rem(rep, n)
    pz = rep // n
    width = heads * hsize
    wrows = width // 128
    gw = 2 * state
    grows = gw // 128
    piece = events * hsize // n
    per_event = n // events
    base = slots + 1
    taps = ikern_ref.shape[0]
    tail = taps - 1

    def to(r):
        return {"rep": r}

    right = lax.rem(rep + 1, total)
    left = lax.rem(rep + total - 1, total)

    loads = [pltpu.make_async_copy(scan_hbm, pool.at[0:slots], load_sem.at[0])]
    for i, (cand, pos) in enumerate(((cand_a, py), (cand_b, pz))):
        loads.append(pltpu.make_async_copy(pscan_hbm.at[:, i * n + pos], cand.at[pos], load_sem.at[1 + i]))
    for copy in loads:
        copy.start()

    barrier = pltpu.get_barrier_semaphore()
    for d in range(1, n):
        pl.semaphore_signal(barrier, inc=1, device_id=to(pz * n + lax.rem(py + d, n)), device_id_type=MESH)
        pl.semaphore_signal(barrier, inc=1, device_id=to(lax.rem(pz + d, n) * n + py), device_id_type=MESH)
    pl.semaphore_signal(barrier, inc=1, device_id=to(right), device_id_type=MESH)
    pl.semaphore_signal(barrier, inc=1, device_id=to(left), device_id_type=MESH)

    pkf[...] = jnp.zeros_like(pkf)
    moved = mv_ref[0]

    def pack(slot, inner_rows, group_rows):
        for tap in range(tail):
            for j in range(wrows):
                pkf[slot, tap * wrows + j : tap * wrows + j + 1, :] = inner_rows[tap][:, j * 128 : (j + 1) * 128]
            for j in range(grows):
                r = tail * wrows + tap * grows + j
                pkf[slot, r : r + 1, :] = group_rows[tap][:, j * 128 : (j + 1) * 128]

    p_inner = [pinner_ref[tap].astype(F32) for tap in range(tail)]
    p_group = [pgroup_ref[tap].astype(F32) for tap in range(tail)]
    for q in range(pref):
        pack(q, [v[q : q + 1] for v in p_inner], [v[q : q + 1] for v in p_group])
    m_inner = cinner_ref[moved].astype(F32)
    m_group = cgroup_ref[moved].astype(F32)
    pack(pref, [m_inner[t : t + 1] for t in range(tail)], [m_group[t : t + 1] for t in range(tail)])
    pkb[...] = pkf[...].astype(BF16)

    pl.semaphore_wait(barrier, 2 * (n - 1) + 2)

    def copy_to(src, dst, send, recv, device):
        return pltpu.make_async_remote_copy(
            src_ref=src, dst_ref=dst, send_sem=send, recv_sem=recv, device_id=to(device), device_id_type=MESH
        )

    streams = (
        Stream(0, n, py, pz, lambda j: pz * n + j, lambda k: k * n + py,
               cand_a, red_a, cand2_a, candc_a, redc_a, candc2_a, conv_a, None),
        Stream(1, n, pz, py, lambda j: j * n + py, lambda k: pz * n + k,
               cand_b, red_b, cand2_b, candc_b, redc_b, candc2_b, conv_b, None),
    )

    def owner(st, e):
        rid = ep_ref[e]
        r = rid // pref
        y, z = lax.rem(r, n), r // n
        return (y, z, lax.rem(rid, pref)) if st.index == 0 else (z, y, lax.rem(rid, pref))

    def half(i):
        return slice(i * 16, (i + 1) * 16)

    def conv1_copy(st, src_pos):
        return copy_to(
            pkb.at[0:pref, half(st.index)], st.candc.at[src_pos],
            sc1.at[st.index], rc1.at[st.index, src_pos - 1], st.peer1(0),
        )

    for st in streams:
        @pl.when(st.pos1 != 0)
        def _(st=st):
            for src in range(1, n):
                @pl.when(st.pos1 == src)
                def _(src=src):
                    conv1_copy(st, src).start()

    def rs1_copy(st, d):
        j = lax.rem(st.pos1 + d, n)
        return copy_to(
            pscan_hbm.at[:, st.index * n + j], st.cand.at[st.pos1],
            s1.at[st.index, d - 1], r1.at[st.index, d - 1], st.peer1(j),
        )

    def rs1_wait(st, d):
        j = lax.rem(st.pos1 + n - d, n)
        copy_to(
            st.cand.at[j], st.cand.at[j], s1.at[st.index, d - 1], r1.at[st.index, d - 1], st.peer1(j)
        ).wait_recv()

    for d in (n // 2, *[x for k in range(n // 2 - 1, 0, -1) for x in (k, n - k)]):
        for st in streams:
            rs1_copy(st, d).start()

    loads[0].wait()
    for h in range(heads):
        got = pool[0, h]
        for s in range(1, slots):
            got = jnp.where(moved == s, pool[s, h], got)
        stage[h] = got
    move_copies = (
        copy_to(pkb.at[pref], camec, sm.at[0], rm.at[0], right),
        copy_to(stage, pool.at[slots], sm.at[1], rm.at[1], right),
    )
    for copy in move_copies:
        copy.start()

    join[...] = jnp.zeros_like(join)
    joing[...] = jnp.zeros_like(joing)
    dts[...] = jnp.zeros_like(dts)
    for t in range(steps):
        join[tail + t, 0:slots, :] = inner_ref[t].astype(F32)
        joing[tail + t, 0:slots, :] = group_ref[t].astype(F32)
        dts[t, 0:slots, :] = dt_ref[t]
    for s in range(slots):
        ucf[s, :, 0:width] = cinner_ref[s].astype(F32)
        ucf[s, :, width : width + gw] = cgroup_ref[s].astype(F32)
    step = []
    decay = []
    for t in range(steps):
        v = dts[t] + dbias_ref[...]
        v = jnp.maximum(v, 0.0) + jnp.log1p(jnp.exp(-jnp.abs(v)))
        step.append(v)
        fall = -v * decay_ref[...]
        decay.append(fall if t == 0 else decay[-1] + fall)

    def conv2_copy(st, k):
        return copy_to(
            st.redc.at[k], st.candc2.at[st.pos2],
            sc2.at[st.index, k], rc2.at[st.index, st.pos2], st.peer2(k),
        )

    def conv_two(st):
        @pl.when(st.pos1 == 0)
        def _():
            for src in range(1, n):
                conv1_copy(st, src).wait_recv()
            st.candc[0] = pkb[0:pref, half(st.index)]
            for e in range(events):
                p, _, row = owner(st, e)
                st.redc[e] = st.candc[p, row]
            for k in range(events):
                @pl.when(st.pos2 != k)
                def _(k=k):
                    conv2_copy(st, k).start()

                @pl.when(st.pos2 == k)
                def _(k=k):
                    st.candc2[k] = st.redc[k]

    def conv3_copy(st, d, e):
        k = lax.rem(st.pos2 + d, n)
        return copy_to(
            st.conv.at[e], st.conv.at[e], sc3.at[st.index, d - 1], rc3.at[st.index, e], st.peer2(k)
        )

    def conv_three(st):
        @pl.when(st.pos1 == 0)
        def _():
            for e in range(events):
                @pl.when(st.pos2 == e)
                def _(e=e):
                    for src in range(n):
                        if src != e:
                            copy_to(
                                st.candc2.at[src], st.candc2.at[src], sc2.at[st.index, 0],
                                rc2.at[st.index, src], st.peer2(src),
                            ).wait_recv()
                    _, q, _ = owner(st, e)
                    st.conv[e] = st.candc2[q]
                    for d in range(1, n):
                        conv3_copy(st, d, e).start()

    def conv4_copy(st, d):
        j = lax.rem(st.pos1 + d, n)
        return copy_to(st.conv, st.conv, sc4.at[st.index, d - 1], rc4.at[st.index], st.peer1(j))

    def conv_four(st):
        @pl.when(st.pos1 == 0)
        def _():
            for e in range(events):
                @pl.when(st.pos2 != e)
                def _(e=e):
                    conv3_copy(st, 1, e).wait_recv()
            for d in range(1, n):
                conv4_copy(st, d).start()

    def conv_five(st):
        @pl.when(st.pos1 != 0)
        def _():
            copy_to(st.conv, st.conv, sc4.at[st.index, 0], rc4.at[st.index], st.peer1(0)).wait_recv()

    def rs2_copy(st, d):
        k = lax.rem(st.pos2 + d, n)
        return copy_to(
            st.red.at[k], st.cand2.at[st.pos2], s2.at[st.index, d - 1], r2.at[st.index, d - 1], st.peer2(k)
        )

    def rs_two(st):
        for d in range(1, n):
            rs1_wait(st, d)
        loads[1 + st.index].wait()
        for e in range(events):
            p, _, row = owner(st, e)
            for u in range(per_event):
                st.red[e * per_event + u] = st.cand[p, row, u * piece : (u + 1) * piece, :]
        for d in range(1, n):
            rs2_copy(st, d).start()
        st.cand2[st.pos2] = st.red[st.pos2]

    def place(head, k):
        return pool.at[base + k // per_event, head, pl.ds(pl.multiple_of(lax.rem(k, per_event) * piece, piece), piece)]

    def ag1_copy(st, d):
        k = lax.rem(st.pos2 + d, n)
        spot = place(st.index * n + st.pos1, st.pos2)
        return copy_to(spot, spot, s3.at[st.index, d - 1], r3.at[st.index, d - 1], st.peer2(k))

    def ag1_wait(st, d):
        k = lax.rem(st.pos2 + n - d, n)
        spot = place(st.index * n + st.pos1, k)
        copy_to(spot, spot, s3.at[st.index, d - 1], r3.at[st.index, d - 1], st.peer2(k)).wait_recv()

    def ag_one(st):
        for d in range(1, n):
            k = lax.rem(st.pos2 + n - d, n)
            copy_to(
                st.cand2.at[k], st.cand2.at[k], s2.at[st.index, d - 1], r2.at[st.index, d - 1], st.peer2(k)
            ).wait_recv()
        _, q, _ = owner(st, st.pos2 // per_event)
        place(st.index * n + st.pos1, st.pos2)[...] = st.cand2[q]
        for d in range(1, n):
            ag1_copy(st, d).start()

    def ring_copy(st, s, way):
        first, last = base, base + events
        if s == n // 2 - 1:
            middle = base + events // 2
            first, last = (first, middle) if way == 0 else (middle, last)
        if way == 0:
            chunk, target = lax.rem(st.pos1 + n - s, n), lax.rem(st.pos1 + 1, n)
        else:
            chunk, target = lax.rem(st.pos1 + s, n), lax.rem(st.pos1 + n - 1, n)
        spot = pool.at[first:last, st.index * n + chunk]
        return copy_to(spot, spot, s4.at[st.index, way, s], r4.at[st.index, way, s], st.peer1(target))

    def ring_wait(st, s, way):
        first, last = base, base + events
        if s == n // 2 - 1:
            middle = base + events // 2
            first, last = (first, middle) if way == 0 else (middle, last)
        chunk = lax.rem(st.pos1 + (n - 1 - s if way == 0 else s + 1), n)
        spot = pool.at[first:last, st.index * n + chunk]
        copy_to(spot, spot, s4.at[st.index, way, s], r4.at[st.index, way, s], st.peer1(chunk)).wait_recv()

    for st in streams:
        conv_two(st)
    for st in streams:
        rs_two(st)
    for st in streams:
        conv_three(st)
    for st in streams:
        ag_one(st)
    for st in streams:
        conv_four(st)
    for st in streams:
        for d in range(1, n):
            ag1_wait(st, d)
        for way in range(2):
            ring_copy(st, 0, way).start()

    for st in streams:
        conv_five(st)
    move_copies[0].wait_recv()
    sources = [(base + e, e) for e in range(events)]

    def unpack(row, top, bottom):
        both = (top.astype(F32), bottom.astype(F32))
        for tap in range(tail):
            for j in range(wrows):
                r = tap * wrows + j
                ucf[row, tap : tap + 1, j * 128 : (j + 1) * 128] = both[r // 16][r % 16 : r % 16 + 1]
            for j in range(grows):
                r = tail * wrows + tap * grows + j
                ucf[row, tap : tap + 1, width + j * 128 : width + (j + 1) * 128] = both[r // 16][r % 16 : r % 16 + 1]

    for row, e in sources:
        unpack(row, conv_a[e], conv_b[e])
    unpack(slots, camec[0:16], camec[16:32])

    index = []
    for s in range(slots):
        e = se_ref[s]
        at = jnp.where(e >= 0, base + e, jnp.where(moved == s, slots, s))
        index.append(at)
        rows = ucf[at]
        for tap in range(tail):
            join[tap, s : s + 1, :] = rows[tap : tap + 1, 0:width]
            joing[tap, s : s + 1, :] = rows[tap : tap + 1, width : width + gw]

    for st in streams:
        for way in range(2):
            ring_wait(st, 0, way)
            ring_copy(st, 1, way).start()

    for t in range(steps):
        v = ibias_ref[...].astype(F32)
        g = gbias_ref[...].astype(F32)
        for k in range(taps):
            v = v + ikern_ref[k : k + 1, :].astype(F32) * join[t + k]
            g = g + gkern_ref[k : k + 1, :].astype(F32) * joing[t + k]
        xs[t] = silu(v)
        gs[t] = silu(g)

    which = lax.broadcasted_iota(jnp.int32, (heads, width), 1) // hsize
    expand = (which == lax.broadcasted_iota(jnp.int32, (heads, width), 0)).astype(BF16)

    def widen(v):
        high, low = split2(v)
        return jnp.dot(high, expand, preferred_element_type=F32) + jnp.dot(low, expand, preferred_element_type=F32)

    for t in range(steps):
        c = gs[t, :, state:gw]
        for s in range(t + 1):
            dot = jnp.sum(c * gs[s, :, 0:state], axis=-1, keepdims=True)
            m = (step[s] if s == t else jnp.exp(decay[t] - decay[s]) * step[s]) * dot
            ms[s] = m + skip_ref[...] if s == t else m
        ms[t + 1] = jnp.exp(decay[t])
        ms[t + 2] = jnp.exp(decay[steps - 1] - decay[t]) * step[t]
        rows = ms[0 : t + 3].reshape(((t + 3) * 8, heads))
        wide = widen(rows).reshape((t + 3, 8, width))
        y = wide[0] * xs[0]
        for s in range(1, t + 1):
            y = y + wide[s] * xs[s]
        ys[t] = y
        es[t] = wide[t + 1]
        us[t] = wide[t + 2] * xs[t]

    for s in range(1, n // 2 - 1):
        for st in streams:
            for way in range(2):
                ring_wait(st, s, way)
                ring_copy(st, s + 1, way).start()

    eye = lax.broadcasted_iota(jnp.int32, (heads, heads), 0) == lax.broadcasted_iota(jnp.int32, (heads, heads), 1)
    last = jnp.exp(decay[steps - 1])
    diag = jnp.concatenate([jnp.where(eye, last[s : s + 1], 0.0) for s in range(slots)], axis=0)
    kept = jnp.dot(diag, jnp.ones((heads, state), F32), precision=lax.Precision.HIGHEST, preferred_element_type=F32)

    for st in streams:
        for way in range(2):
            ring_wait(st, n // 2 - 1, way)
    move_copies[1].wait_recv()

    pad = jnp.zeros((16 - steps, state), F32)
    padw = jnp.zeros((16 - steps, width), F32)
    for s in range(slots):
        start = pool[index[s]].reshape((width, state))
        c_high, c_low = split2(jnp.concatenate([gs[:, s, state:gw], pad], axis=0))
        read = lax.dot_general(
            jnp.concatenate([c_high, c_low], axis=0), start, (((1,), (1,)), ((), ())), preferred_element_type=F32
        )
        read = read[0:steps] + read[16 : 16 + steps]
        ys[:, s, :] = ys[:, s, :] + es[:, s, :] * read
        b_high, b_low = split2(jnp.concatenate([gs[:, s, 0:state], pad], axis=0))
        u_high, u_low = split2(jnp.concatenate([us[:, s, :], padw], axis=0))
        added = lax.dot_general(
            jnp.concatenate([u_high, u_low, u_high], axis=0),
            jnp.concatenate([b_high, b_high, b_low], axis=0),
            (((0,), (0,)), ((), ())), preferred_element_type=F32,
        )
        for h in range(heads):
            rows = slice(h * hsize, (h + 1) * hsize)
            k = s * heads + h
            fin_ref[s, h] = (kept[k : k + 1] * start[rows].astype(F32) + added[rows]).astype(BF16)

    for t in range(steps):
        y = ys[t, 0:slots, :] * silu(gate_ref[t].astype(F32))
        mean = jnp.sum(y * y, axis=-1, keepdims=True) / width
        out_ref[t] = (y * lax.rsqrt(mean + EPSILON) * gain_ref[...]).astype(BF16)

    for st in streams:
        @pl.when(st.pos1 != 0)
        def _(st=st):
            conv1_copy(st, 1).wait_send()

        @pl.when(st.pos1 == 0)
        def _(st=st):
            for k in range(events):
                @pl.when(st.pos2 != k)
                def _(k=k):
                    conv2_copy(st, k).wait_send()

                @pl.when(st.pos2 == k)
                def _(k=k):
                    for d in range(1, n):
                        conv3_copy(st, d, k).wait_send()
            for d in range(1, n):
                conv4_copy(st, d).wait_send()

        for d in range(1, n):
            rs1_copy(st, d).wait_send()
            rs2_copy(st, d).wait_send()
            ag1_copy(st, d).wait_send()
        for s in range(n // 2):
            for way in range(2):
                ring_copy(st, s, way).wait_send()
    for copy in move_copies:
        copy.wait_send()


def on_device(
    n,
    inner_input, group_input, gate_input, step_size, scan_state, conv_inner, conv_group,
    prefix_scan, prefix_inner, prefix_group, inner_kernel, inner_bias, group_kernel, group_bias,
    decay_rate, step_bias, skip_gain, norm_gain, event_prefix, slot_event, moved_slot,
):
    slots, steps, width = inner_input.shape
    pref, heads, hsize, state = prefix_scan.shape
    events = event_prefix.shape[0]
    taps = inner_kernel.shape[0]
    tail = taps - 1
    gw = group_input.shape[-1]
    piece = events * hsize // n
    final_inner = inner_input[:, steps - tail :]
    final_group = group_input[:, steps - tail :]

    args = (
        inner_input.transpose(1, 0, 2),
        group_input.reshape(slots, steps, gw).transpose(1, 0, 2),
        gate_input.transpose(1, 0, 2),
        step_size.transpose(1, 0, 2),
        scan_state,
        conv_inner,
        conv_group.reshape(slots, tail, gw),
        prefix_scan,
        prefix_inner.transpose(1, 0, 2),
        prefix_group.reshape(pref, tail, gw).transpose(1, 0, 2),
        inner_kernel,
        inner_bias.reshape(1, width),
        group_kernel.reshape(taps, gw),
        group_bias.reshape(1, gw),
        decay_rate.reshape(1, heads),
        step_bias.reshape(1, heads),
        skip_gain.reshape(1, heads),
        norm_gain.reshape(1, width),
        event_prefix,
        slot_event,
        moved_slot,
    )
    vmem = pl.BlockSpec(memory_space=pltpu.VMEM)
    smem = pl.BlockSpec(memory_space=pltpu.SMEM)
    hbm = pl.BlockSpec(memory_space=pl.ANY)
    specs = [vmem] * len(args)
    specs[4] = specs[7] = hbm
    specs[-3:] = [smem] * 3
    dma = pltpu.SemaphoreType.DMA
    block = (hsize, state)
    scratch = [
        pltpu.VMEM((slots + 1 + events, heads) + block, BF16),
        pltpu.VMEM((heads,) + block, BF16),
        pltpu.VMEM((n, pref) + block, BF16),
        pltpu.VMEM((n, pref) + block, BF16),
        pltpu.VMEM((n, piece, state), BF16),
        pltpu.VMEM((n, piece, state), BF16),
        pltpu.VMEM((n, piece, state), BF16),
        pltpu.VMEM((n, piece, state), BF16),
        pltpu.VMEM((pref + 1, 32, 128), F32),
        pltpu.VMEM((pref + 1, 32, 128), BF16),
        pltpu.VMEM((n, pref, 16, 128), BF16),
        pltpu.VMEM((n, pref, 16, 128), BF16),
        pltpu.VMEM((events, 16, 128), BF16),
        pltpu.VMEM((events, 16, 128), BF16),
        pltpu.VMEM((n, 16, 128), BF16),
        pltpu.VMEM((n, 16, 128), BF16),
        pltpu.VMEM((events, 16, 128), BF16),
        pltpu.VMEM((events, 16, 128), BF16),
        pltpu.VMEM((32, 128), BF16),
        pltpu.VMEM((slots + 1 + events, tail, width + gw), F32),
        pltpu.VMEM((steps + tail, 8, width), F32),
        pltpu.VMEM((steps + tail, 8, gw), F32),
        pltpu.VMEM((steps, 8, width), F32),
        pltpu.VMEM((steps, 8, gw), F32),
        pltpu.VMEM((steps, 8, heads), F32),
        pltpu.VMEM((steps + 2, 8, heads), F32),
        pltpu.VMEM((steps, 8, width), F32),
        pltpu.VMEM((steps, 8, width), F32),
        pltpu.VMEM((steps, 8, width), F32),
        dma((3,)),
        dma((2, n - 1)), dma((2, n - 1)),
        dma((2, n - 1)), dma((2, n - 1)),
        dma((2, n - 1)), dma((2, n - 1)),
        dma((2, 2, n // 2)), dma((2, 2, n // 2)),
        dma((2,)), dma((2, n - 1)),
        dma((2, events)), dma((2, n)),
        dma((2, n - 1)), dma((2, events)),
        dma((2, n - 1)), dma((2,)),
        dma((2,)), dma((2,)),
    ]
    layer, final_scan = pl.pallas_call(
        functools.partial(kernel, n, slots, pref, events, steps, heads, hsize, state),
        out_shape=(
            jax.ShapeDtypeStruct((steps, slots, width), BF16),
            jax.ShapeDtypeStruct(scan_state.shape, BF16),
        ),
        in_specs=specs,
        out_specs=(vmem, vmem),
        scratch_shapes=scratch,
        compiler_params=pltpu.CompilerParams(
            collective_id=0, has_side_effects=True, vmem_limit_bytes=40 * 1024 * 1024
        ),
    )(*args)
    return layer.transpose(1, 0, 2), final_scan, final_inner, final_group


def solution(mesh):
    count = mesh.shape["rep"]
    n = 1
    while n * n < count:
        n += 1
    placed = (
        P("rep", None, "ch"),
        P("rep", None, "ch", None),
        P("rep", None, "ch"),
        P("rep", None, "ch"),
        P("rep", "ch", None, None),
        P("rep", None, "ch"),
        P("rep", None, "ch", None),
        P("rep", "ch", None, None),
        P("rep", None, "ch"),
        P("rep", None, "ch", None),
        P(None, "ch"),
        P("ch"),
        P(None, "ch", None),
        P("ch", None),
        P("ch"),
        P("ch"),
        P("ch"),
        P("ch"),
        P(),
        P("rep"),
        P("rep"),
    )
    return jax.shard_map(
        functools.partial(on_device, n),
        mesh=mesh,
        in_specs=placed,
        out_specs=(
            P("rep", None, "ch"),
            P("rep", "ch", None, None),
            P("rep", None, "ch"),
            P("rep", None, "ch", None),
        ),
        check_vma=False,
    )
```

time: 430 us -> 76.4 us (0.18)
  blocking collectives: 281 us -> 0 us
  matrix products: 73.4 us -> 0 us
  Pallas kernels: 0 us -> 55.9 us
  other arithmetic: 27 us -> 0 us
  between operations: 26.3 us -> 1.33 us
  starting transfers between devices: 10.5 us -> 0 us
  local copies, waits for them, and re-layouts: 10.5 us -> 18.5 us
    psum x1 -> x0, blocking collectives: 281 us -> none  [from_root(): return lax.psum(kept, axis)]
    dot_general x10 -> x0, matrix products: 73.4 us -> none  [run_scan(): jnp.einsum('shpn,shn->shp', carried, readout, precision=lax.Precision.HIG...]
    pallas_call x0 -> x1, Pallas kernels: none -> 55.9 us  [on_device(): pl.pallas_call(functools.partial(kernel, n, slots, pref, events, steps, h...]
    unnamed x129 -> x42, local copies, waits for them, and re-layouts: 2.27 us -> 17.8 us
    convert_element_type x9 -> x0, other arithmetic: 15 us -> none  [the longest x1 14 us: on_device(): carried.astype(jnp.bfloat16)]
    ppermute x3 -> x0, starting transfers between devices: 10.4 us -> none  [shifted(): return lax.ppermute(x, axis, [(i, (i + by) % count) for i in range(count)])]
    mul x12 -> x0, other arithmetic: 6.54 us -> none  [the longest x10 6.31 us: run_scan(): step_value[:, :, None] * values]
  transfers between devices with their start and end apart: 4 -> 0, of which waited for: 0 -> 0; matrix products, arithmetic and copies ran while one was open for 5% -> 0% of each run, Pallas kernels for 0% -> 0%
where the time goes in v1:
time: 76.4 us; the launch traced here: 75.7 us
  Pallas kernels  55.9 us (73%)
  local copies, waits for them, and re-layouts  18.5 us (24%)
  between operations  1.33 us (2%)
    pallas_call x1, Pallas kernels, on_device(): pl.pallas_call(functools.partial(kernel, n, slots, pref, events, steps, h...  55.9 us
    unnamed x42, local copies, waits for them, and re-layouts  17.8 us

profile of v1, /device:TPU:6, one launch (start us, length us, event | category | flops | bytes accessed | tf_op | source)
XLA Modules:
  0.0 75.7 jit_solution(7140668883107158554)
XLA Ops:
  0.6 0.7 reshape.38.ibias_ref
  2.0 1.4 %copy-done = bf16[6,16,64,128]{3,2,1,0:T(8,128)(2,1)S(1)} copy-done((bf16[6,16,64,128]{3,2,1,0:T(8,128)(2,1)S(1)}, bf16[6,16,64,128]{3,2,1,0:T(8,128)(2,1)}, u32[]{:S(2)}) %copy-start) | copy-done | bytes 1572888
  3.4 1.0 %copy-done.1 = bf16[2,16,64,128]{3,2,1,0:T(8,128)(2,1)S(1)} copy-done((bf16[2,16,64,128]{3,2,1,0:T(8,128)(2,1)S(1)}, bf16[2,16,64,128]{3,2,1,0:T(8,128)(2,1)}, u32[]{:S(2)}) %copy-start.1) | copy-done | bytes 524312
  4.4 0.9 %copy-done.2 = bf16[6,10,1024]{2,0,1:T(8,128)(2,1)S(1)} copy-done((bf16[6,10,1024]{2,0,1:T(8,128)(2,1)S(1)}, bf16[6,10,1024]{2,0,1:T(8,128)(2,1)}, u32[]{:S(2)}) %copy-start.2) | copy-done | bytes 122904
  5.3 0.9 %copy-done.3 = bf16[6,10,1024]{2,0,1:T(8,128)(2,1)S(1)} copy-done((bf16[6,10,1024]{2,0,1:T(8,128)(2,1)S(1)}, bf16[6,10,1024]{2,0,1:T(8,128)(2,1)}, u32[]{:S(2)}) %copy-start.3) | copy-done | bytes 122904
  6.3 0.8 %copy-done.4 = bf16[6,10,1,256]{3,0,2,1:T(8,128)(2,1)S(1)} copy-done((bf16[6,10,1,256]{3,0,2,1:T(8,128)(2,1)S(1)}, bf16[6,10,1,256]{3,0,2,1:T(8,128)(2,1)}, u32[]{:S(2)}) %copy-start.4) | copy-done | bytes 30744
  7.0 0.8 %copy-done.5 = bf16[6,3,1024]{2,1,0:T(4,128)(2,1)S(1)} copy-done((bf16[6,3,1024]{2,1,0:T(4,128)(2,1)S(1)}, bf16[6,3,1024]{2,1,0:T(4,128)(2,1)}, u32[]{:S(2)}) %copy-start.5) | copy-done | bytes 36888
  7.8 0.8 %copy-done.6 = f32[6,10,16]{2,0,1:T(8,128)S(1)} copy-done((f32[6,10,16]{2,0,1:T(8,128)S(1)}, f32[6,10,16]{2,0,1:T(8,128)}, u32[]{:S(2)}) %copy-start.6) | copy-done | bytes 3864
  8.6 0.7 copy-done.7
  9.3 0.7 copy-done.8
  10.0 0.7 copy-done.9
  10.7 0.7 copy-done.10
  11.4 0.7 copy-done.11
  12.1 0.7 copy-done.12
  12.8 0.7 copy-done.13
  13.5 0.7 copy-done.14
  14.1 0.7 copy-done.15
  14.8 0.7 copy-done.16
  15.4 0.7 copy-done.17
  16.1 0.7 copy-done.18
  16.7 55.9 %shard_map.228 = (bf16[10,6,1024]{2,1,0:T(8,128)(2,1)S(1)}, bf16[6,16,64,128]{3,2,1,0:T(8,128)(2,1)S(1)}) custom-call(bf16[10,6,1024]{2,1,0:T(8,128)(2,1)S(1)} %bitcast.17, bf16[10,6,256]{2,1,0:T(8,128)(2,1)S(1)} %bitcast.20, bf16[10,6,1024]{2,1,0:T(8,128)(2,1)S(1)} %bitcast.18, f32[10,6,16]{2,1,0:T(8,128)S(1)} %bitcast.21, ...), custom_call_target="tpu_custom_call" | custom-call | tf_op jit(solution)/shard_map/pallas_call | solution.py:559
  72.6 0.7 copy.27
  73.9 0.7 copy.32
  74.6 1.1 %copy.33 = bf16[6,16,64,128]{3,2,1,0:T(8,128)(2,1)} copy(bf16[6,16,64,128]{3,2,1,0:T(8,128)(2,1)S(1)} %get-tuple-element.13) | data formatting | bytes 3145728
  (22 shorter events, 0.6 us)
Async XLA Ops:
  2.0 1.4 %copy-start = (bf16[6,16,64,128]{3,2,1,0:T(8,128)(2,1)S(1)}, bf16[6,16,64,128]{3,2,1,0:T(8,128)(2,1)}, u32[]{:S(2)}) copy-start(bf16[6,16,64,128]{3,2,1,0:T(8,128)(2,1)} %scan_hbm.1) | copy-start | bytes 4718596
  3.4 1.0 %copy-start.1 = (bf16[2,16,64,128]{3,2,1,0:T(8,128)(2,1)S(1)}, bf16[2,16,64,128]{3,2,1,0:T(8,128)(2,1)}, u32[]{:S(2)}) copy-start(bf16[2,16,64,128]{3,2,1,0:T(8,128)(2,1)} %pscan_hbm.1) | copy-start | bytes 1572868
  4.4 0.9 %copy-start.2 = (bf16[6,10,1024]{2,0,1:T(8,128)(2,1)S(1)}, bf16[6,10,1024]{2,0,1:T(8,128)(2,1)}, u32[]{:S(2)}) copy-start(bf16[6,10,1024]{2,0,1:T(8,128)(2,1)} %param.21) | copy-start | bytes 368644
  5.3 0.9 %copy-start.3 = (bf16[6,10,1024]{2,0,1:T(8,128)(2,1)S(1)}, bf16[6,10,1024]{2,0,1:T(8,128)(2,1)}, u32[]{:S(2)}) copy-start(bf16[6,10,1024]{2,0,1:T(8,128)(2,1)} %param.23) | copy-start | bytes 368644
  6.3 0.8 %copy-start.4 = (bf16[6,10,1,256]{3,0,2,1:T(8,128)(2,1)S(1)}, bf16[6,10,1,256]{3,0,2,1:T(8,128)(2,1)}, u32[]{:S(2)}) copy-start(bf16[6,10,1,256]{3,0,2,1:T(8,128)(2,1)} %param.22) | copy-start | bytes 92164
  7.0 0.8 %copy-start.5 = (bf16[6,3,1024]{2,1,0:T(4,128)(2,1)S(1)}, bf16[6,3,1024]{2,1,0:T(4,128)(2,1)}, u32[]{:S(2)}) copy-start(bf16[6,3,1024]{2,1,0:T(4,128)(2,1)} %cinner_ref.1) | copy-start | bytes 110596
  7.8 0.8 %copy-start.6 = (f32[6,10,16]{2,0,1:T(8,128)S(1)}, f32[6,10,16]{2,0,1:T(8,128)}, u32[]{:S(2)}) copy-start(f32[6,10,16]{2,0,1:T(8,128)} %param.24) | copy-start | bytes 11524
  8.6 0.7 copy-start.7
  9.3 0.7 copy-start.8
  10.0 0.7 copy-start.9
  10.7 0.7 copy-start.10
  11.4 0.7 copy-start.11
  12.1 0.7 copy-start.12
  12.8 0.7 copy-start.13
  13.5 0.7 copy-start.14
  14.1 0.7 copy-start.15
  14.8 0.7 copy-start.16
  15.4 0.7 copy-start.17
  16.1 0.7 copy-start.18

commit v2 on v1

v2 whole, which is shorter than its diff:
```python
import functools

import jax
import jax.numpy as jnp
from jax import lax
from jax.experimental import pallas as pl
from jax.experimental.pallas import tpu as pltpu
from jax.sharding import PartitionSpec as P

MESH = pl.DeviceIdType.MESH
BF16 = jnp.bfloat16
F32 = jnp.float32
EPSILON = 1e-05
PARTS = 1
MOVES = (((0, 0), (0, 1)), ((0, 2), (0, 3)), (), ())


def silu(v):
    return v / (1.0 + jnp.exp(-v))


def split2(v):
    high = v.astype(BF16)
    low = (v - high.astype(F32)).astype(BF16)
    return high, low


class Stream:
    def __init__(self, index, pos1, pos2, peer1, peer2, cand, red, cand2, candc, redc, candc2, conv):
        self.index = index
        self.pos1, self.pos2 = pos1, pos2
        self.peer1, self.peer2 = peer1, peer2
        self.cand, self.red, self.cand2 = cand, red, cand2
        self.candc, self.redc, self.candc2 = candc, redc, candc2
        self.conv = conv


def kernel(
    n, parts, slots, pref, events, steps, heads, hsize, state,
    *refs,
):
    inputs, refs = refs[:21], refs[21:]
    (out_ref, fin_ref, finner_ref, fgroup_ref), refs = refs[:4], refs[4:]
    held, refs = refs[:19], refs[19:]
    scan_hbm, pscan_hbm = inputs[4], inputs[7]
    (
        inner_ref, group_ref, gate_ref, dt_ref, cinner_ref, cgroup_ref, pinner_ref, pgroup_ref,
        ikern_ref, ibias_ref, gkern_ref, gbias_ref, decay_ref, dbias_ref, skip_ref, gain_ref, ep_ref, se_ref, mv_ref,
    ) = held
    blocks, refs = refs[: 8 * parts], refs[8 * parts :]
    cands, reds, cand2s = (blocks[2 * parts * i : 2 * parts * (i + 1)] for i in range(3))
    pools, stages = blocks[6 * parts : 7 * parts], blocks[7 * parts :]
    (
        pkf, pkb, candc_a, candc_b, redc_a, redc_b, candc2_a, candc2_b, conv_a, conv_b, camec, ucf,
        join, joing, xs, gs, dts, ms, us, ys, es,
        load_sem, small_sem, s1, r1, s2, r2, s3, r3, s4, r4, sc1, rc1, sc2, rc2, sc3, rc3, sc4, rc4, sm, rm,
    ) = refs
    rep = lax.axis_index("rep")
    total = n * n
    py = lax.rem(rep, n)
    pz = rep // n
    width = heads * hsize
    wrows = width // 128
    gw = 2 * state
    grows = gw // 128
    part = heads * hsize // parts
    share = part // 2
    chunk = share // n
    piece = events * chunk // n
    per_event = n // events
    base = slots + 1
    taps = ikern_ref.shape[0]
    tail = taps - 1

    def to(r):
        return {"rep": r}

    right = lax.rem(rep + 1, total)
    left = lax.rem(rep + total - 1, total)

    barrier = pltpu.get_barrier_semaphore()
    for d in range(1, n):
        pl.semaphore_signal(barrier, inc=1, device_id=to(pz * n + lax.rem(py + d, n)), device_id_type=MESH)
        pl.semaphore_signal(barrier, inc=1, device_id=to(lax.rem(pz + d, n) * n + py), device_id_type=MESH)
    pl.semaphore_signal(barrier, inc=1, device_id=to(right), device_id_type=MESH)
    pl.semaphore_signal(barrier, inc=1, device_id=to(left), device_id_type=MESH)

    def chunk_rows(st, j):
        return pl.ds(pl.multiple_of(st * share + j * chunk, chunk), chunk)

    def all_rows(b, st, j):
        return pl.ds(pl.multiple_of(b * part + st * share + j * chunk, chunk), chunk)

    first = (6, 7, 4, 5, 18)
    rest = [v for i, v in enumerate(inputs) if i not in (4, 7)]
    small = [pltpu.make_async_copy(src, dst, small_sem.at[i]) for i, (src, dst) in enumerate(zip(rest, held))]
    for i in first:
        small[i].start()
    scan_loads = [
        pltpu.make_async_copy(
            scan_hbm.at[:, b * part : (b + 1) * part], pools[b].at[0:slots], load_sem.at[2 * parts + b]
        )
        for b in range(parts)
    ]
    for copy in scan_loads:
        copy.start()
    own_loads = {}
    for b in range(parts):
        for i, pos in enumerate((py, pz)):
            at = i * parts + b
            own_loads[i, b] = pltpu.make_async_copy(
                pscan_hbm.at[:, all_rows(b, i, pos)], cands[at].at[pos], load_sem.at[at]
            )
            own_loads[i, b].start()
    for i, copy in enumerate(small):
        if i not in first:
            copy.start()

    def copy_to(src, dst, send, recv, device):
        return pltpu.make_async_remote_copy(
            src_ref=src, dst_ref=dst, send_sem=send, recv_sem=recv, device_id=to(device), device_id_type=MESH
        )

    streams = (
        Stream(0, py, pz, lambda j: pz * n + j, lambda k: k * n + py,
               cands[:parts], reds[:parts], cand2s[:parts], candc_a, redc_a, candc2_a, conv_a),
        Stream(1, pz, py, lambda j: j * n + py, lambda k: pz * n + k,
               cands[parts:], reds[parts:], cand2s[parts:], candc_b, redc_b, candc2_b, conv_b),
    )

    def owner(st, e):
        rid = ep_ref[e]
        r = rid // pref
        y, z = lax.rem(r, n), r // n
        return (y, z, lax.rem(rid, pref)) if st.index == 0 else (z, y, lax.rem(rid, pref))

    def half(i):
        return slice(i * 16, (i + 1) * 16)

    def conv1_copy(st):
        return copy_to(
            pkb.at[0:pref, half(st.index)], st.candc.at[st.pos1], sc1.at[st.index], rc1.at[st.index], st.peer1(0)
        )

    def taken(ref, sem, way):
        copy = copy_to(ref, ref, sem, sem, right)
        copy.wait_send() if way == 0 else copy.wait_recv()

    def rs1_copy(st, b, d):
        j = lax.rem(st.pos1 + d, n)
        return copy_to(
            pscan_hbm.at[:, all_rows(b, st.index, j)], st.cand[b].at[st.pos1],
            s1.at[st.index, b], r1.at[st.index, b], st.peer1(j),
        )

    far_first = (n // 2, *[x for k in range(n // 2 - 1, 0, -1) for x in (k, n - k)])
    pl.semaphore_wait(barrier, 2 * (n - 1) + 2)

    def rs1_send(b):
        for d in far_first:
            for st in streams:
                rs1_copy(st, b, d).start()

    for b in range(parts):
        rs1_send(b)

    pkf[...] = jnp.zeros_like(pkf)
    for i in first:
        small[i].wait()
    moved = mv_ref[0]

    def pack(slot, inner_rows, group_rows):
        for tap in range(tail):
            for j in range(wrows):
                pkf[slot, tap * wrows + j : tap * wrows + j + 1, :] = inner_rows[tap][:, j * 128 : (j + 1) * 128]
            for j in range(grows):
                r = tail * wrows + tap * grows + j
                pkf[slot, r : r + 1, :] = group_rows[tap][:, j * 128 : (j + 1) * 128]

    p_inner = [pinner_ref[tap].astype(F32) for tap in range(tail)]
    p_group = [pgroup_ref[tap].astype(F32) for tap in range(tail)]
    for q in range(pref):
        pack(q, [v[q : q + 1] for v in p_inner], [v[q : q + 1] for v in p_group])
    m_inner = cinner_ref[moved].astype(F32)
    m_group = cgroup_ref[moved].astype(F32)
    pack(pref, [m_inner[t : t + 1] for t in range(tail)], [m_group[t : t + 1] for t in range(tail)])
    pkb[...] = pkf[...].astype(BF16)

    for st in streams:
        @pl.when(st.pos1 != 0)
        def _(st=st):
            conv1_copy(st).start()

    for b in range(parts):
        scan_loads[b].wait()
        for q in range(0, part, hsize):
            rows = slice(q, q + hsize)
            got = pools[b][0, rows]
            for s in range(1, slots):
                got = jnp.where(moved == s, pools[b][s, rows], got)
            stages[b][rows] = got
    conv_move = copy_to(pkb.at[pref], camec, sm.at[parts], rm.at[parts], right)
    conv_move.start()

    def move(b, i, count):
        rows = pl.ds(i * part // count, part // count)
        return copy_to(stages[b].at[rows], pools[b].at[slots, rows], sm.at[b], rm.at[b], right)

    for i, copy in enumerate(small):
        if i not in first:
            copy.wait()
    join[...] = jnp.zeros_like(join)
    joing[...] = jnp.zeros_like(joing)
    dts[...] = jnp.zeros_like(dts)
    for t in range(steps):
        join[tail + t, 0:slots, :] = inner_ref[t].astype(F32)
        joing[tail + t, 0:slots, :] = group_ref[t].astype(F32)
        if t >= steps - tail:
            for s in range(slots):
                k = t - (steps - tail)
                finner_ref[s, k : k + 1, :] = inner_ref[t, s : s + 1, :]
                fgroup_ref[s, k : k + 1, :] = group_ref[t, s : s + 1, :]
        dts[t, 0:slots, :] = dt_ref[t]
    for s in range(slots):
        ucf[s, :, 0:width] = cinner_ref[s].astype(F32)
        ucf[s, :, width : width + gw] = cgroup_ref[s].astype(F32)
    step = []
    decay = []
    for t in range(steps):
        v = dts[t] + dbias_ref[...]
        v = jnp.maximum(v, 0.0) + jnp.log1p(jnp.exp(-jnp.abs(v)))
        step.append(v)
        fall = -v * decay_ref[...]
        decay.append(fall if t == 0 else decay[-1] + fall)

    def conv2_copy(st, k):
        return copy_to(
            st.redc.at[k], st.candc2.at[st.pos2], sc2.at[st.index], rc2.at[st.index], st.peer2(k)
        )

    def conv_two(st):
        @pl.when(st.pos1 == 0)
        def _():
            taken(st.candc.at[1:n], rc1.at[st.index], 1)
            st.candc[0] = pkb[0:pref, half(st.index)]
            for e in range(events):
                p, _, row = owner(st, e)
                st.redc[e] = st.candc[p, row]
            for k in range(events):
                @pl.when(st.pos2 != k)
                def _(k=k):
                    conv2_copy(st, k).start()

                @pl.when(st.pos2 == k)
                def _(k=k):
                    st.candc2[k] = st.redc[k]

    def conv3_copy(st, d, e):
        k = lax.rem(st.pos2 + d, n)
        return copy_to(st.conv.at[e], st.conv.at[e], sc3.at[st.index], rc3.at[st.index], st.peer2(k))

    def conv_three(st):
        @pl.when(st.pos1 == 0)
        def _():
            for e in range(events):
                @pl.when(st.pos2 == e)
                def _(e=e):
                    taken(st.candc2.at[0 : n - 1], rc2.at[st.index], 1)
                    _, q, _ = owner(st, e)
                    st.conv[e] = st.candc2[q]
                    for d in range(1, n):
                        conv3_copy(st, d, e).start()

    def conv4_copy(st, d):
        j = lax.rem(st.pos1 + d, n)
        return copy_to(st.conv, st.conv, sc4.at[st.index], rc4.at[st.index], st.peer1(j))

    def conv_four(st):
        @pl.when(st.pos1 == 0)
        def _():
            @pl.when(st.pos2 < events)
            def _():
                taken(st.conv.at[0 : events - 1], rc3.at[st.index], 1)

            @pl.when(st.pos2 >= events)
            def _():
                taken(st.conv, rc3.at[st.index], 1)

            for d in range(1, n):
                conv4_copy(st, d).start()

    def conv_five(st):
        @pl.when(st.pos1 != 0)
        def _():
            taken(st.conv, rc4.at[st.index], 1)

    def rs2_copy(st, b, d):
        k = lax.rem(st.pos2 + d, n)
        return copy_to(
            st.red[b].at[k], st.cand2[b].at[st.pos2], s2.at[st.index, b], r2.at[st.index, b], st.peer2(k)
        )

    def rs_two(st, b):
        taken(st.cand[b].at[0 : n - 1], r1.at[st.index, b], 1)
        own_loads[st.index, b].wait()
        for e in range(events):
            p, _, row = owner(st, e)
            for u in range(per_event):
                st.red[b][e * per_event + u] = st.cand[b][p, row, u * piece : (u + 1) * piece, :]
        for d in far_first:
            rs2_copy(st, b, d).start()
        st.cand2[b][st.pos2] = st.red[b][st.pos2]

    def place(b, st, j, k):
        offset = pl.multiple_of(st.index * share + j * chunk + lax.rem(k, per_event) * piece, piece)
        return pools[b].at[base + k // per_event, pl.ds(offset, piece)]

    def ag1_copy(st, b, d):
        spot = place(b, st, st.pos1, st.pos2)
        return copy_to(spot, spot, s3.at[st.index, b], r3.at[st.index, b], st.peer2(lax.rem(st.pos2 + d, n)))

    def ag_one(st, b):
        taken(st.cand2[b].at[0 : n - 1], r2.at[st.index, b], 1)
        _, q, _ = owner(st, st.pos2 // per_event)
        place(b, st, st.pos1, st.pos2)[...] = st.cand2[b][q]
        for d in far_first:
            ag1_copy(st, b, d).start()

    pair = events // 2
    whole = (0, events)
    first_leg = [(0, 2) + whole, (0, -2) + whole, (0, 1) + whole, (0, -1) + whole]
    second_leg = [(-2, 2, 0, pair), (-2, 1) + whole, (2, -2, pair, events), (2, -1) + whole]
    if n == 4:
        first_leg = [(0, 2, 0, pair), (0, -2, pair, events), (0, 1) + whole, (0, -1) + whole]
        second_leg = []
    legs = first_leg + second_leg

    def leg_spot(st, b, distance, first, last):
        j = lax.rem(st.pos1 + n + distance, n)
        return pools[b].at[base + first : base + last, chunk_rows(st.index, j)]

    def leg_send(st, b, some):
        for i in some:
            c, t, a, z = legs[i]
            spot = leg_spot(st, b, c, a, z)
            target = st.peer1(lax.rem(st.pos1 + n + t, n))
            copy_to(spot, spot, s4.at[st.index, b], r4.at[st.index, b, i], target).start()

    def leg_wait(st, b, some):
        for i in some:
            c, t, a, z = legs[i]
            taken(leg_spot(st, b, c - t, a, z), r4.at[st.index, b, i], 1)

    def spread(st, b):
        taken(st.cand2[b].at[0 : n - 1], r3.at[st.index, b], 1)
        leg_send(st, b, range(4))

    def hand_on(b):
        if second_leg:
            for way in range(2):
                for st in streams:
                    leg_wait(st, b, [way])
                    leg_send(st, b, [4 + 2 * way, 5 + 2 * way])

    def arrive(b):
        for st in streams:
            leg_wait(st, b, range(2 if second_leg else 0, len(legs)))

    def each(phase, b):
        for st in streams:
            phase(st, b)

    def conv(phase):
        for st in streams:
            phase(st)

    def moves(when):
        for b, i in MOVES[when]:
            move(b, i, 4 // parts).start()

    for when, (phase, conv_phase) in enumerate(((rs_two, conv_two), (ag_one, conv_three), (spread, conv_four))):
        for b in range(parts):
            each(phase, b)
            if b == 0:
                conv(conv_phase)
        moves(when)
    for b in range(parts):
        hand_on(b)
    moves(3)
    conv(conv_five)
    conv_move.wait_recv()
    sources = [(base + e, e) for e in range(events)]

    def unpack(row, top, bottom):
        both = (top.astype(F32), bottom.astype(F32))
        for tap in range(tail):
            for j in range(wrows):
                r = tap * wrows + j
                ucf[row, tap : tap + 1, j * 128 : (j + 1) * 128] = both[r // 16][r % 16 : r % 16 + 1]
            for j in range(grows):
                r = tail * wrows + tap * grows + j
                ucf[row, tap : tap + 1, width + j * 128 : width + (j + 1) * 128] = both[r // 16][r % 16 : r % 16 + 1]

    for row, e in sources:
        unpack(row, conv_a[e], conv_b[e])
    unpack(slots, camec[0:16], camec[16:32])

    index = []
    for s in range(slots):
        e = se_ref[s]
        at = jnp.where(e >= 0, base + e, jnp.where(moved == s, slots, s))
        index.append(at)
        rows = ucf[at]
        for tap in range(tail):
            join[tap, s : s + 1, :] = rows[tap : tap + 1, 0:width]
            joing[tap, s : s + 1, :] = rows[tap : tap + 1, width : width + gw]


    for t in range(steps):
        v = ibias_ref[...].astype(F32).reshape(1, width)
        g = gbias_ref[...].astype(F32)
        for k in range(taps):
            v = v + ikern_ref[k : k + 1, :].astype(F32) * join[t + k]
            g = g + gkern_ref[k : k + 1, :].astype(F32) * joing[t + k]
        xs[t] = silu(v)
        gs[t] = silu(g)

    which = lax.broadcasted_iota(jnp.int32, (heads, width), 1) // hsize
    expand = (which == lax.broadcasted_iota(jnp.int32, (heads, width), 0)).astype(BF16)

    def widen(v):
        high, low = split2(v)
        return jnp.dot(high, expand, preferred_element_type=F32) + jnp.dot(low, expand, preferred_element_type=F32)

    for t in range(steps):
        c = gs[t, :, state:gw]
        for s in range(t + 1):
            dot = jnp.sum(c * gs[s, :, 0:state], axis=-1, keepdims=True)
            m = (step[s] if s == t else jnp.exp(decay[t] - decay[s]) * step[s]) * dot
            ms[s] = m + skip_ref[...] if s == t else m
        ms[t + 1] = jnp.exp(decay[t])
        ms[t + 2] = jnp.exp(decay[steps - 1] - decay[t]) * step[t]
        rows = ms[0 : t + 3].reshape(((t + 3) * 8, heads))
        wide = widen(rows).reshape((t + 3, 8, width))
        y = wide[0] * xs[0]
        for s in range(1, t + 1):
            y = y + wide[s] * xs[s]
        ys[t] = y
        es[t] = wide[t + 1]
        us[t] = wide[t + 2] * xs[t]

    eye = lax.broadcasted_iota(jnp.int32, (heads, heads), 0) == lax.broadcasted_iota(jnp.int32, (heads, heads), 1)
    last = jnp.exp(decay[steps - 1])
    diag = jnp.concatenate([jnp.where(eye, last[s : s + 1], 0.0) for s in range(slots)], axis=0)
    kept = jnp.dot(diag, jnp.ones((heads, state), F32), precision=lax.Precision.HIGHEST, preferred_element_type=F32)

    pad = jnp.zeros((16 - steps, state), F32)
    padw = jnp.zeros((16 - steps, part), F32)
    for b in range(parts):
        arrive(b)
        taken(stages[b], rm.at[b], 1)
        lanes = slice(b * part, (b + 1) * part)
        for s in range(slots):
            start = pools[b][index[s]]
            c_high, c_low = split2(jnp.concatenate([gs[:, s, state:gw], pad], axis=0))
            read = lax.dot_general(
                jnp.concatenate([c_high, c_low], axis=0), start, (((1,), (1,)), ((), ())), preferred_element_type=F32
            )
            read = read[0:steps] + read[16 : 16 + steps]
            ys[:, s, lanes] = ys[:, s, lanes] + es[:, s, lanes] * read
            b_high, b_low = split2(jnp.concatenate([gs[:, s, 0:state], pad], axis=0))
            u_high, u_low = split2(jnp.concatenate([us[:, s, lanes], padw], axis=0))
            added = lax.dot_general(
                jnp.concatenate([u_high, u_low, u_high], axis=0),
                jnp.concatenate([b_high, b_high, b_low], axis=0),
                (((0,), (0,)), ((), ())), preferred_element_type=F32,
            )
            for q in range(part // hsize):
                rows = slice(q * hsize, (q + 1) * hsize)
                h = b * (part // hsize) + q
                k = s * heads + h
                fin_ref[s, h] = (kept[k : k + 1] * start[rows].astype(F32) + added[rows]).astype(BF16)

    for t in range(steps):
        y = ys[t, 0:slots, :] * silu(gate_ref[t].astype(F32))
        mean = jnp.sum(y * y, axis=-1, keepdims=True) / width
        out_ref[t] = (y * lax.rsqrt(mean + EPSILON) * gain_ref[...]).astype(BF16)

    for st in streams:
        @pl.when(st.pos1 != 0)
        def _(st=st):
            conv1_copy(st).wait_send()

        @pl.when(st.pos1 == 0)
        def _(st=st):
            @pl.when(st.pos2 < events)
            def _():
                taken(st.conv.at[0 : events - 1], sc2.at[st.index], 0)
                taken(st.candc2.at[0 : n - 1], sc3.at[st.index], 0)

            @pl.when(st.pos2 >= events)
            def _():
                taken(st.conv, sc2.at[st.index], 0)

            taken(pools[0].at[base, 0 : (n - 1) * events * 16], sc4.at[st.index], 0)

        for b in range(parts):
            taken(st.cand[b].at[0 : n - 1], s1.at[st.index, b], 0)
            taken(st.red[b].at[0 : n - 1], s2.at[st.index, b], 0)
            taken(st.red[b].at[0 : n - 1], s3.at[st.index, b], 0)
            taken(pools[b].at[base : base + events, 0 : (n - 1) * chunk], s4.at[st.index, b], 0)
    conv_move.wait_send()
    for b in range(parts):
        taken(stages[b], sm.at[b], 0)


def finish(*refs):
    half = len(refs) // 2
    copies = [pltpu.make_async_copy(a, b, refs[-1].at[i]) for i, (a, b) in enumerate(zip(refs[:half], refs[half:-1]))]
    for copy in copies:
        copy.start()
    for copy in copies:
        copy.wait()


def on_device(
    n,
    inner_input, group_input, gate_input, step_size, scan_state, conv_inner, conv_group,
    prefix_scan, prefix_inner, prefix_group, inner_kernel, inner_bias, group_kernel, group_bias,
    decay_rate, step_bias, skip_gain, norm_gain, event_prefix, slot_event, moved_slot,
):
    slots, steps, width = inner_input.shape
    pref, heads, hsize, state = prefix_scan.shape
    events = event_prefix.shape[0]
    taps = inner_kernel.shape[0]
    tail = taps - 1
    gw = group_input.shape[-1]
    part = heads * hsize // PARTS
    chunk = part // (2 * n)
    piece = events * chunk // n

    args = (
        inner_input.transpose(1, 0, 2),
        group_input.reshape(slots, steps, gw).transpose(1, 0, 2),
        gate_input.transpose(1, 0, 2),
        step_size.transpose(1, 0, 2),
        scan_state.reshape(slots, width, state),
        conv_inner,
        conv_group.reshape(slots, tail, gw),
        prefix_scan.reshape(pref, width, state),
        prefix_inner.transpose(1, 0, 2),
        prefix_group.reshape(pref, tail, gw).transpose(1, 0, 2),
        inner_kernel,
        inner_bias,
        group_kernel.reshape(taps, gw),
        group_bias.reshape(1, gw),
        decay_rate.reshape(1, heads),
        step_bias.reshape(1, heads),
        skip_gain.reshape(1, heads),
        norm_gain.reshape(1, width),
        event_prefix,
        slot_event,
        moved_slot,
    )
    vmem = pl.BlockSpec(memory_space=pltpu.VMEM)
    hbm = pl.BlockSpec(memory_space=pl.ANY)
    specs = [hbm] * len(args)
    small = [v for i, v in enumerate(args) if i not in (4, 7)]
    args = tuple(v if v.size == 1 else pltpu.with_memory_space_constraint(v, pltpu.HBM) for v in args)
    dma = pltpu.SemaphoreType.DMA
    scratch = [(pltpu.VMEM if i < len(small) - 3 else pltpu.SMEM)(v.shape, v.dtype) for i, v in enumerate(small)]
    scratch += [
        *[pltpu.VMEM((n, pref, chunk, state), BF16)] * (2 * PARTS),
        *[pltpu.VMEM((n, piece, state), BF16)] * (4 * PARTS),
        *[pltpu.VMEM((slots + 1 + events, part, state), BF16)] * PARTS,
        *[pltpu.VMEM((part, state), BF16)] * PARTS,
        pltpu.VMEM((pref + 1, 32, 128), F32),
        pltpu.VMEM((pref + 1, 32, 128), BF16),
        pltpu.VMEM((n, pref, 16, 128), BF16),
        pltpu.VMEM((n, pref, 16, 128), BF16),
        pltpu.VMEM((events, 16, 128), BF16),
        pltpu.VMEM((events, 16, 128), BF16),
        pltpu.VMEM((n, 16, 128), BF16),
        pltpu.VMEM((n, 16, 128), BF16),
        pltpu.VMEM((events, 16, 128), BF16),
        pltpu.VMEM((events, 16, 128), BF16),
        pltpu.VMEM((32, 128), BF16),
        pltpu.VMEM((slots + 1 + events, tail, width + gw), F32),
        pltpu.VMEM((steps + tail, 8, width), F32),
        pltpu.VMEM((steps + tail, 8, gw), F32),
        pltpu.VMEM((steps, 8, width), F32),
        pltpu.VMEM((steps, 8, gw), F32),
        pltpu.VMEM((steps, 8, heads), F32),
        pltpu.VMEM((steps + 2, 8, heads), F32),
        pltpu.VMEM((steps, 8, width), F32),
        pltpu.VMEM((steps, 8, width), F32),
        pltpu.VMEM((steps, 8, width), F32),
        dma((3 * PARTS,)), dma((len(small),)),
        *[dma((2, PARTS))] * 7, dma((2, PARTS, 8)),
        *[dma((2,))] * 8,
        *[dma((PARTS + 1,))] * 2,
    ]
    shapes = (
        jax.ShapeDtypeStruct((steps, slots, width), BF16),
        jax.ShapeDtypeStruct(scan_state.shape, BF16),
        jax.ShapeDtypeStruct((slots, tail, width), BF16),
        jax.ShapeDtypeStruct((slots, tail, gw), BF16),
    )
    results = pl.pallas_call(
        functools.partial(kernel, n, PARTS, slots, pref, events, steps, heads, hsize, state),
        out_shape=shapes,
        in_specs=specs,
        out_specs=(vmem,) * 4,
        scratch_shapes=scratch,
        compiler_params=pltpu.CompilerParams(
            collective_id=0, has_side_effects=True, vmem_limit_bytes=40 * 1024 * 1024
        ),
    )(*args)
    layer, final_scan, final_inner, final_group = pl.pallas_call(
        finish,
        out_shape=shapes,
        in_specs=[hbm] * 4,
        out_specs=(hbm,) * 4,
        scratch_shapes=[dma((4,))],
        compiler_params=pltpu.CompilerParams(vmem_limit_bytes=40 * 1024 * 1024),
    )(*results)
    return layer.transpose(1, 0, 2), final_scan, final_inner, final_group.reshape(slots, tail, 1, gw)


def solution(mesh):
    count = mesh.shape["rep"]
    n = 1
    while n * n < count:
        n += 1
    placed = (
        P("rep", None, "ch"),
        P("rep", None, "ch", None),
        P("rep", None, "ch"),
        P("rep", None, "ch"),
        P("rep", "ch", None, None),
        P("rep", None, "ch"),
        P("rep", None, "ch", None),
        P("rep", "ch", None, None),
        P("rep", None, "ch"),
        P("rep", None, "ch", None),
        P(None, "ch"),
        P("ch"),
        P(None, "ch", None),
        P("ch", None),
        P("ch"),
        P("ch"),
        P("ch"),
        P("ch"),
        P(),
        P("rep"),
        P("rep"),
    )
    return jax.shard_map(
        functools.partial(on_device, n),
        mesh=mesh,
        in_specs=placed,
        out_specs=(
            P("rep", None, "ch"),
            P("rep", "ch", None, None),
            P("rep", None, "ch"),
            P("rep", None, "ch", None),
        ),
        check_vma=False,
    )
```

time: 76.4 us -> 45.8 us (0.60)
  local copies, waits for them, and re-layouts: 18.5 us -> 0 us
  Pallas kernels: 55.9 us -> 44.3 us
    unnamed x42 -> x0, local copies, waits for them, and re-layouts: 17.8 us -> none
    pallas_call x1 -> x2, Pallas kernels: 55.9 us -> 44.3 us  [the longest x1 43.1 us: on_device(): pl.pallas_call(functools.partial(kernel, n, PARTS, slots, pref, events, s...]
where the time goes in v2:
time: 45.8 us; the launch traced here: 45.6 us
  Pallas kernels  44.3 us (97%)
  between operations  1.29 us (3%)
    pallas_call x1, Pallas kernels, on_device(): pl.pallas_call(functools.partial(kernel, n, PARTS, slots, pref, events, s...  43.1 us
    pallas_call x1, Pallas kernels, on_device(): pl.pallas_call(finish, out_shape=shapes, in_specs=[hbm] * 4, out_specs=(h...  1.24 us

profile of v2, /device:TPU:6, one launch (start us, length us, event | category | flops | bytes accessed | tf_op | source)
XLA Modules:
  0.0 45.6 jit_solution(3331953229219465479)
XLA Ops:
  1.3 43.1 %shard_map.228 = (bf16[10,6,1024]{2,1,0:T(8,128)(2,1)S(1)}, bf16[6,16,64,128]{3,2,1,0:T(8,128)(2,1)S(1)}, bf16[6,3,1024]{2,1,0:T(4,128)(2,1)S(1)}, bf16[6,3,256]{2,1,0:T(4,128)(2,1)S(1)}) custom-call(bf16[10,6,1024]{2,1,0:T(8,128)(2,1)} %bitcast.24, bf16[10,6,256]{2,1,0:T(8,128)(2,1)} %bitcast.26, bf16[10,6,1024]{2,1,0:T(8,128)(2,1)} %bitcast.25, ...), custom_call_target="tpu_custom_call" | custom-call | tf_op jit(solution)/shard_map/pallas_call | solution.py:609
  44.4 1.2 %shard_map.229 = (bf16[10,6,1024]{2,1,0:T(8,128)(2,1)}, bf16[6,16,64,128]{3,2,1,0:T(8,128)(2,1)}, bf16[6,3,1024]{2,1,0:T(4,128)(2,1)}, bf16[6,3,256]{2,1,0:T(4,128)(2,1)}) custom-call(bf16[10,6,1024]{2,1,0:T(8,128)(2,1)S(1)} %get-tuple-element.12.refs_0_, bf16[6,16,64,128]{3,2,1,0:T(8,128)(2,1)S(1)} %get-tuple-element.13.refs_1_, ...), custom_call_target="tpu_custom_call" | custom-call | tf_op jit(solution)/shard_map/pallas_call | solution.py:619

commit v3 on v2

--- a/solution.py
+++ b/solution.py
@@ -52,7 +52,7 @@
     pools, stages = blocks[6 * parts : 7 * parts], blocks[7 * parts :]
     (
         pkf, pkb, candc_a, candc_b, redc_a, redc_b, candc2_a, candc2_b, conv_a, conv_b, camec, ucf,
-        join, joing, xs, gs, dts, ms, us, ys, es,
+        join, joing, xs, gs, dts, ms, us, ys, es, added,
         load_sem, small_sem, s1, r1, s2, r2, s3, r3, s4, r4, sc1, rc1, sc2, rc2, sc3, rc3, sc4, rc4, sm, rm,
     ) = refs
     rep = lax.axis_index("rep")
@@ -79,7 +79,7 @@
     left = lax.rem(rep + total - 1, total)
 
     barrier = pltpu.get_barrier_semaphore()
-    for d in range(1, n):
+    for d in (n // 2, *[x for k in range(n // 2 - 1, 0, -1) for x in (k, n - k)]):
         pl.semaphore_signal(barrier, inc=1, device_id=to(pz * n + lax.rem(py + d, n)), device_id_type=MESH)
         pl.semaphore_signal(barrier, inc=1, device_id=to(lax.rem(pz + d, n) * n + py), device_id_type=MESH)
     pl.semaphore_signal(barrier, inc=1, device_id=to(right), device_id_type=MESH)
@@ -327,11 +327,12 @@
             ag1_copy(st, b, d).start()
 
     pair = events // 2
-    whole = (0, events)
-    first_leg = [(0, 2) + whole, (0, -2) + whole, (0, 1) + whole, (0, -1) + whole]
-    second_leg = [(-2, 2, 0, pair), (-2, 1) + whole, (2, -2, pair, events), (2, -1) + whole]
+    low, high, whole = (0, pair), (pair, events), (0, events)
+    first_leg = [(0, 2) + low, (0, -2) + low, (0, 2) + high, (0, -2) + high, (0, 1) + whole, (0, -1) + whole]
+    second_leg = [(-2, 2) + low, (-2, 1) + low, (2, -1) + low, (-2, 1) + high, (2, -2) + high, (2, -1) + high]
+    handed = ((6, 7), (8,), (9,), (10, 11))
     if n == 4:
-        first_leg = [(0, 2, 0, pair), (0, -2, pair, events), (0, 1) + whole, (0, -1) + whole]
+        first_leg = [(0, 2) + low, (0, -2) + high, (0, 1) + whole, (0, -1) + whole]
         second_leg = []
     legs = first_leg + second_leg
 
@@ -353,18 +354,18 @@
 
     def spread(st, b):
         taken(st.cand2[b].at[0 : n - 1], r3.at[st.index, b], 1)
-        leg_send(st, b, range(4))
+        leg_send(st, b, range(len(first_leg)))
 
     def hand_on(b):
         if second_leg:
-            for way in range(2):
+            for i, some in enumerate(handed):
                 for st in streams:
-                    leg_wait(st, b, [way])
-                    leg_send(st, b, [4 + 2 * way, 5 + 2 * way])
+                    leg_wait(st, b, [i])
+                    leg_send(st, b, some)
 
     def arrive(b):
         for st in streams:
-            leg_wait(st, b, range(2 if second_leg else 0, len(legs)))
+            leg_wait(st, b, range(len(handed) if second_leg else 0, len(legs)))
 
     def each(phase, b):
         for st in streams:
@@ -455,34 +456,37 @@
     kept = jnp.dot(diag, jnp.ones((heads, state), F32), precision=lax.Precision.HIGHEST, preferred_element_type=F32)
 
     pad = jnp.zeros((16 - steps, state), F32)
-    padw = jnp.zeros((16 - steps, part), F32)
+    padw = jnp.zeros((16 - steps, width), F32)
+    reads = []
+    for s in range(slots):
+        c_high, c_low = split2(jnp.concatenate([gs[:, s, state:gw], pad], axis=0))
+        reads.append(jnp.concatenate([c_high, c_low], axis=0))
+        b_high, b_low = split2(jnp.concatenate([gs[:, s, 0:state], pad], axis=0))
+        u_high, u_low = split2(jnp.concatenate([us[:, s, :], padw], axis=0))
+        added[s] = lax.dot_general(
+            jnp.concatenate([u_high, u_low, u_high], axis=0),
+            jnp.concatenate([b_high, b_high, b_low], axis=0),
+            (((0,), (0,)), ((), ())), preferred_element_type=F32,
+        )
+    for t in range(steps):
+        join[t, 0:slots, :] = silu(gate_ref[t].astype(F32))
     for b in range(parts):
         arrive(b)
         taken(stages[b], rm.at[b], 1)
         lanes = slice(b * part, (b + 1) * part)
         for s in range(slots):
             start = pools[b][index[s]]
-            c_high, c_low = split2(jnp.concatenate([gs[:, s, state:gw], pad], axis=0))
-            read = lax.dot_general(
-                jnp.concatenate([c_high, c_low], axis=0), start, (((1,), (1,)), ((), ())), preferred_element_type=F32
-            )
+            read = lax.dot_general(reads[s], start, (((1,), (1,)), ((), ())), preferred_element_type=F32)
             read = read[0:steps] + read[16 : 16 + steps]
             ys[:, s, lanes] = ys[:, s, lanes] + es[:, s, lanes] * read
-            b_high, b_low = split2(jnp.concatenate([gs[:, s, 0:state], pad], axis=0))
-            u_high, u_low = split2(jnp.concatenate([us[:, s, lanes], padw], axis=0))
-            added = lax.dot_general(
-                jnp.concatenate([u_high, u_low, u_high], axis=0),
-                jnp.concatenate([b_high, b_high, b_low], axis=0),
-                (((0,), (0,)), ((), ())), preferred_element_type=F32,
-            )
             for q in range(part // hsize):
                 rows = slice(q * hsize, (q + 1) * hsize)
                 h = b * (part // hsize) + q
                 k = s * heads + h
-                fin_ref[s, h] = (kept[k : k + 1] * start[rows].astype(F32) + added[rows]).astype(BF16)
+                fin_ref[s, h] = (kept[k : k + 1] * start[rows].astype(F32) + added[s, b * part + q * hsize : b * part + (q + 1) * hsize]).astype(BF16)
 
     for t in range(steps):
-        y = ys[t, 0:slots, :] * silu(gate_ref[t].astype(F32))
+        y = ys[t, 0:slots, :] * join[t, 0:slots, :]
         mean = jnp.sum(y * y, axis=-1, keepdims=True) / width
         out_ref[t] = (y * lax.rsqrt(mean + EPSILON) * gain_ref[...]).astype(BF16)
 
@@ -516,7 +520,11 @@
 
 def finish(*refs):
     half = len(refs) // 2
-    copies = [pltpu.make_async_copy(a, b, refs[-1].at[i]) for i, (a, b) in enumerate(zip(refs[:half], refs[half:-1]))]
+    pairs = list(zip(refs[:half], refs[half:-1]))
+    layer, scan, inner, group = pairs
+    pairs = [(v.at[i], w.at[i]) for v, w in (scan,) for i in range(v.shape[0])]
+    pairs += [layer, inner, group]
+    copies = [pltpu.make_async_copy(v, w, refs[-1].at[i]) for i, (v, w) in enumerate(pairs)]
     for copy in copies:
         copy.start()
     for copy in copies:
@@ -595,8 +603,9 @@
         pltpu.VMEM((steps, 8, width), F32),
         pltpu.VMEM((steps, 8, width), F32),
         pltpu.VMEM((steps, 8, width), F32),
+        pltpu.VMEM((slots, width, state), F32),
         dma((3 * PARTS,)), dma((len(small),)),
-        *[dma((2, PARTS))] * 7, dma((2, PARTS, 8)),
+        *[dma((2, PARTS))] * 7, dma((2, PARTS, 12)),
         *[dma((2,))] * 8,
         *[dma((PARTS + 1,))] * 2,
     ]
@@ -621,7 +630,7 @@
         out_shape=shapes,
         in_specs=[hbm] * 4,
         out_specs=(hbm,) * 4,
-        scratch_shapes=[dma((4,))],
+        scratch_shapes=[dma((slots + 3,))],
         compiler_params=pltpu.CompilerParams(vmem_limit_bytes=40 * 1024 * 1024),
     )(*results)
     return layer.transpose(1, 0, 2), final_scan, final_inner, final_group.reshape(slots, tail, 1, gw)

time: 45.8 us -> 45.7 us (level)
  no operation moved by 1% of the time
where the time goes in v3:
time: 45.7 us; the launch traced here: 45.6 us
  Pallas kernels  44.3 us (97%)
  between operations  1.29 us (3%)
    pallas_call x1, Pallas kernels, on_device(): pl.pallas_call(functools.partial(kernel, n, PARTS, slots, pref, events, s...  43 us
    pallas_call x1, Pallas kernels, on_device(): pl.pallas_call(finish, out_shape=shapes, in_specs=[hbm] * 4, out_specs=(h...  1.27 us

profile of v3, /device:TPU:6, one launch (start us, length us, event | category | flops | bytes accessed | tf_op | source)
XLA Modules:
  0.0 45.6 jit_solution(4193714893194333124)
XLA Ops:
  1.3 43.0 %shard_map.228 = (bf16[10,6,1024]{2,1,0:T(8,128)(2,1)S(1)}, bf16[6,16,64,128]{3,2,1,0:T(8,128)(2,1)S(1)}, bf16[6,3,1024]{2,1,0:T(4,128)(2,1)S(1)}, bf16[6,3,256]{2,1,0:T(4,128)(2,1)S(1)}) custom-call(bf16[10,6,1024]{2,1,0:T(8,128)(2,1)} %bitcast.24, bf16[10,6,256]{2,1,0:T(8,128)(2,1)} %bitcast.26, bf16[10,6,1024]{2,1,0:T(8,128)(2,1)} %bitcast.25, ...), custom_call_target="tpu_custom_call" | custom-call | tf_op jit(solution)/shard_map/pallas_call | solution.py:618
  44.3 1.3 %shard_map.229 = (bf16[10,6,1024]{2,1,0:T(8,128)(2,1)}, bf16[6,16,64,128]{3,2,1,0:T(8,128)(2,1)}, bf16[6,3,1024]{2,1,0:T(4,128)(2,1)}, bf16[6,3,256]{2,1,0:T(4,128)(2,1)}) custom-call(bf16[10,6,1024]{2,1,0:T(8,128)(2,1)S(1)} %get-tuple-element.12.refs_0_, bf16[6,16,64,128]{3,2,1,0:T(8,128)(2,1)S(1)} %get-tuple-element.13.refs_1_, ...), custom_call_target="tpu_custom_call" | custom-call | tf_op jit(solution)/shard_map/pallas_call | solution.py:628

commit v4 on v3

--- a/solution.py
+++ b/solution.py
@@ -12,7 +12,7 @@
 F32 = jnp.float32
 EPSILON = 1e-05
 PARTS = 1
-MOVES = (((0, 0), (0, 1)), ((0, 2), (0, 3)), (), ())
+MOVES = (((0, 0), (0, 1)), ((1, 0), (1, 1)), (), ())
 
 
 def silu(v):
@@ -47,9 +47,9 @@
         inner_ref, group_ref, gate_ref, dt_ref, cinner_ref, cgroup_ref, pinner_ref, pgroup_ref,
         ikern_ref, ibias_ref, gkern_ref, gbias_ref, decay_ref, dbias_ref, skip_ref, gain_ref, ep_ref, se_ref, mv_ref,
     ) = held
-    blocks, refs = refs[: 8 * parts], refs[8 * parts :]
+    blocks, refs = refs[: 6 * parts + 4], refs[6 * parts + 4 :]
     cands, reds, cand2s = (blocks[2 * parts * i : 2 * parts * (i + 1)] for i in range(3))
-    pools, stages = blocks[6 * parts : 7 * parts], blocks[7 * parts :]
+    pools, stages = blocks[6 * parts : 6 * parts + 2], blocks[6 * parts + 2 :]
     (
         pkf, pkb, candc_a, candc_b, redc_a, redc_b, candc2_a, candc2_b, conv_a, conv_b, camec, ucf,
         join, joing, xs, gs, dts, ms, us, ys, es, added,
@@ -98,9 +98,9 @@
         small[i].start()
     scan_loads = [
         pltpu.make_async_copy(
-            scan_hbm.at[:, b * part : (b + 1) * part], pools[b].at[0:slots], load_sem.at[2 * parts + b]
+            scan_hbm.at[:, b * share : (b + 1) * share], pools[b].at[0:slots], load_sem.at[2 * parts + b]
         )
-        for b in range(parts)
+        for b in range(2)
     ]
     for copy in scan_loads:
         copy.start()
@@ -191,19 +191,19 @@
         def _(st=st):
             conv1_copy(st).start()
 
-    for b in range(parts):
+    for b in range(2):
         scan_loads[b].wait()
-        for q in range(0, part, hsize):
+        for q in range(0, share, hsize):
             rows = slice(q, q + hsize)
             got = pools[b][0, rows]
             for s in range(1, slots):
                 got = jnp.where(moved == s, pools[b][s, rows], got)
             stages[b][rows] = got
-    conv_move = copy_to(pkb.at[pref], camec, sm.at[parts], rm.at[parts], right)
+    conv_move = copy_to(pkb.at[pref], camec, sm.at[2], rm.at[2], right)
     conv_move.start()
 
     def move(b, i, count):
-        rows = pl.ds(i * part // count, part // count)
+        rows = pl.ds(i * share // count, share // count)
         return copy_to(stages[b].at[rows], pools[b].at[slots, rows], sm.at[b], rm.at[b], right)
 
     for i, copy in enumerate(small):
@@ -312,8 +312,8 @@
         st.cand2[b][st.pos2] = st.red[b][st.pos2]
 
     def place(b, st, j, k):
-        offset = pl.multiple_of(st.index * share + j * chunk + lax.rem(k, per_event) * piece, piece)
-        return pools[b].at[base + k // per_event, pl.ds(offset, piece)]
+        offset = pl.multiple_of(j * chunk + lax.rem(k, per_event) * piece, piece)
+        return pools[st.index].at[base + k // per_event, pl.ds(offset, piece)]
 
     def ag1_copy(st, b, d):
         spot = place(b, st, st.pos1, st.pos2)
@@ -338,7 +338,7 @@
 
     def leg_spot(st, b, distance, first, last):
         j = lax.rem(st.pos1 + n + distance, n)
-        return pools[b].at[base + first : base + last, chunk_rows(st.index, j)]
+        return pools[st.index].at[base + first : base + last, chunk_rows(0, j)]
 
     def leg_send(st, b, some):
         for i in some:
@@ -363,8 +363,8 @@
                     leg_wait(st, b, [i])
                     leg_send(st, b, some)
 
-    def arrive(b):
-        for st in streams:
+    def arrive(st):
+        for b in range(parts):
             leg_wait(st, b, range(len(handed) if second_leg else 0, len(legs)))
 
     def each(phase, b):
@@ -377,7 +377,7 @@
 
     def moves(when):
         for b, i in MOVES[when]:
-            move(b, i, 4 // parts).start()
+            move(b, i, 2).start()
 
     for when, (phase, conv_phase) in enumerate(((rs_two, conv_two), (ag_one, conv_three), (spread, conv_four))):
         for b in range(parts):
@@ -470,20 +470,20 @@
         )
     for t in range(steps):
         join[t, 0:slots, :] = silu(gate_ref[t].astype(F32))
-    for b in range(parts):
-        arrive(b)
+    for b in range(2):
+        arrive(streams[b])
         taken(stages[b], rm.at[b], 1)
-        lanes = slice(b * part, (b + 1) * part)
+        lanes = slice(b * share, (b + 1) * share)
         for s in range(slots):
             start = pools[b][index[s]]
             read = lax.dot_general(reads[s], start, (((1,), (1,)), ((), ())), preferred_element_type=F32)
             read = read[0:steps] + read[16 : 16 + steps]
             ys[:, s, lanes] = ys[:, s, lanes] + es[:, s, lanes] * read
-            for q in range(part // hsize):
+            for q in range(share // hsize):
                 rows = slice(q * hsize, (q + 1) * hsize)
-                h = b * (part // hsize) + q
+                h = b * (share // hsize) + q
                 k = s * heads + h
-                fin_ref[s, h] = (kept[k : k + 1] * start[rows].astype(F32) + added[s, b * part + q * hsize : b * part + (q + 1) * hsize]).astype(BF16)
+                fin_ref[s, h] = (kept[k : k + 1] * start[rows].astype(F32) + added[s, b * share + q * hsize : b * share + (q + 1) * hsize]).astype(BF16)
 
     for t in range(steps):
         y = ys[t, 0:slots, :] * join[t, 0:slots, :]
@@ -512,9 +512,9 @@
             taken(st.cand[b].at[0 : n - 1], s1.at[st.index, b], 0)
             taken(st.red[b].at[0 : n - 1], s2.at[st.index, b], 0)
             taken(st.red[b].at[0 : n - 1], s3.at[st.index, b], 0)
-            taken(pools[b].at[base : base + events, 0 : (n - 1) * chunk], s4.at[st.index, b], 0)
+            taken(pools[st.index].at[base : base + events, 0 : (n - 1) * chunk], s4.at[st.index, b], 0)
     conv_move.wait_send()
-    for b in range(parts):
+    for b in range(2):
         taken(stages[b], sm.at[b], 0)
 
 
@@ -580,8 +580,8 @@
     scratch += [
         *[pltpu.VMEM((n, pref, chunk, state), BF16)] * (2 * PARTS),
         *[pltpu.VMEM((n, piece, state), BF16)] * (4 * PARTS),
-        *[pltpu.VMEM((slots + 1 + events, part, state), BF16)] * PARTS,
-        *[pltpu.VMEM((part, state), BF16)] * PARTS,
+        *[pltpu.VMEM((slots + 1 + events, part // 2, state), BF16)] * 2,
+        *[pltpu.VMEM((part // 2, state), BF16)] * 2,
         pltpu.VMEM((pref + 1, 32, 128), F32),
         pltpu.VMEM((pref + 1, 32, 128), BF16),
         pltpu.VMEM((n, pref, 16, 128), BF16),
@@ -604,10 +604,10 @@
         pltpu.VMEM((steps, 8, width), F32),
         pltpu.VMEM((steps, 8, width), F32),
         pltpu.VMEM((slots, width, state), F32),
-        dma((3 * PARTS,)), dma((len(small),)),
+        dma((2 * PARTS + 2,)), dma((len(small),)),
         *[dma((2, PARTS))] * 7, dma((2, PARTS, 12)),
         *[dma((2,))] * 8,
-        *[dma((PARTS + 1,))] * 2,
+        *[dma((3,))] * 2,
     ]
     shapes = (
         jax.ShapeDtypeStruct((steps, slots, width), BF16),

time: 45.7 us -> 45.5 us (level)
  no operation moved by 1% of the time
where the time goes in v4:
time: 45.5 us; the launch traced here: 45.3 us
  Pallas kernels  44 us (97%)
  between operations  1.29 us (3%)
    pallas_call x1, Pallas kernels, on_device(): pl.pallas_call(functools.partial(kernel, n, PARTS, slots, pref, events, s...  42.8 us
    pallas_call x1, Pallas kernels, on_device(): pl.pallas_call(finish, out_shape=shapes, in_specs=[hbm] * 4, out_specs=(h...  1.27 us

profile of v4, /device:TPU:6, one launch (start us, length us, event | category | flops | bytes accessed | tf_op | source)
XLA Modules:
  0.0 45.3 jit_solution(12586211024945597227)
XLA Ops:
  1.3 42.8 %shard_map.228 = (bf16[10,6,1024]{2,1,0:T(8,128)(2,1)S(1)}, bf16[6,16,64,128]{3,2,1,0:T(8,128)(2,1)S(1)}, bf16[6,3,1024]{2,1,0:T(4,128)(2,1)S(1)}, bf16[6,3,256]{2,1,0:T(4,128)(2,1)S(1)}) custom-call(bf16[10,6,1024]{2,1,0:T(8,128)(2,1)} %bitcast.24, bf16[10,6,256]{2,1,0:T(8,128)(2,1)} %bitcast.26, bf16[10,6,1024]{2,1,0:T(8,128)(2,1)} %bitcast.25, ...), custom_call_target="tpu_custom_call" | custom-call | tf_op jit(solution)/shard_map/pallas_call | solution.py:618
  44.1 1.3 %shard_map.229 = (bf16[10,6,1024]{2,1,0:T(8,128)(2,1)}, bf16[6,16,64,128]{3,2,1,0:T(8,128)(2,1)}, bf16[6,3,1024]{2,1,0:T(4,128)(2,1)}, bf16[6,3,256]{2,1,0:T(4,128)(2,1)}) custom-call(bf16[10,6,1024]{2,1,0:T(8,128)(2,1)S(1)} %get-tuple-element.12.refs_0_, bf16[6,16,64,128]{3,2,1,0:T(8,128)(2,1)S(1)} %get-tuple-element.13.refs_1_, ...), custom_call_target="tpu_custom_call" | custom-call | tf_op jit(solution)/shard_map/pallas_call | solution.py:628
